TPU v7x, 512 devices: a whole 4x8x8 slice. The times are simulated.
512 devices in a mesh: ctx: 64 (over y, x, core), head: 8 (over z).
Axes of the slice: x: 4, y: 8, z: 8, core: 2. Of those that a mesh axis runs over, the one named last changes fastest.
Arguments:
- x_prompt: bfloat16 [32768, 4096], P('ctx', 'head'), may hold values from -6 to 6
- norm_gain: bfloat16 [4096], replicated, may hold values from 0.25 to 1.75
- key_weight: bfloat16 [4096, 4096], P('ctx', 'head'), may hold values from -0.09375 to 0.09375
- value_weight: bfloat16 [4096, 4096], P('ctx', 'head'), may hold values from -0.09375 to 0.09375
- cache_keys: bfloat16 [32768, 4096], P('ctx', 'head'), may hold values from -6 to 6
- cache_values: bfloat16 [32768, 4096], P('ctx', 'head'), may hold values from -6 to 6
- resp_queries: bfloat16 [512, 4096], P('ctx', 'head'), may hold values from -270 to 270
- resp_keys: bfloat16 [512, 4096], P('ctx', 'head'), may hold values from -6 to 6
- resp_values: bfloat16 [512, 4096], P('ctx', 'head'), may hold values from -6 to 6
- drift_ids: int32 [64, 4], replicated, may hold values from 0 to 3, as said below
- drift_count: int32 [64], replicated, may hold values from 0 to 4, as said below
Outputs:
- new_keys: bfloat16 [32768, 4096], P('ctx', 'head')
- new_values: bfloat16 [32768, 4096], P('ctx', 'head')
- attended: bfloat16 [512, 4096], P('ctx', 'head')
Inputs may be any that keep to these rules, and one draw needn't show every extreme that they name: `drift_ids`: each row s holds distinct block numbers of shard s; entries at or beyond drift_count[s] are ignored. `drift_count`: some shard has exactly 4 drifted blocks.
All inputs are finite; a program needn't handle non-finite values.
Results may differ from a plain program's by a relative error of at most 0.0078.
Values may be sent and summed in bfloat16 or wider, within the bound.
No kernel may reach another device: no remote copies, remote signals or barrier semaphores. Data moves between devices by JAX's collectives and lax.ppermute only.
A program may use at most 64 MiB of HBM per device.

v0:
```python
import jax
import jax.numpy as jnp
from jax import lax
from jax.sharding import PartitionSpec as P

HD = 128
BLOCK = 128


eps = 1e-05


def normalize(rows, gain):
    values = rows.astype(jnp.float32)
    scale = lax.rsqrt(jnp.mean(values * values, axis=1, keepdims=True) + eps)
    return (values * scale * gain.astype(jnp.float32)[None, :]).astype(jnp.bfloat16)


def body(
    x_prompt,
    norm_gain,
    key_weight,
    value_weight,
    cache_keys,
    cache_values,
    resp_queries,
    resp_keys,
    resp_values,
    drift_ids,
    drift_count,
):
    block = BLOCK
    slot_total = drift_ids.shape[1]
    slice_width = x_prompt.shape[1]
    blocks_dev = cache_keys.shape[0] // block
    here = lax.axis_index("ctx")
    mine_ids = lax.dynamic_index_in_dim(drift_ids, here, 0, keepdims=False)
    count_me = lax.dynamic_index_in_dim(drift_count, here, 0, keepdims=False)
    shaped = x_prompt.reshape(blocks_dev, block, slice_width)
    own_rows = jnp.take(shaped, mine_ids, axis=0).reshape(slot_total * block, slice_width)

    def slot_of(task):
        return jnp.where(task < count_me, task, slot_total + task - count_me)

    full_rows = lax.all_gather(own_rows, "head", axis=1, tiled=True)
    normed = normalize(full_rows, norm_gain)
    width = key_weight.shape[1]
    empty = jnp.zeros((full_rows.shape[0], width), jnp.float32)
    whole_k, whole_v = (
        lax.all_gather(key_weight, "ctx", axis=0, tiled=True),
        lax.all_gather(value_weight, "ctx", axis=0, tiled=True),
    )

    def compute(task, sums):
        slot = slot_of(task)
        part = lax.dynamic_slice_in_dim(normed, slot * block, block, 0)
        made_k = jnp.dot(part, whole_k, preferred_element_type=jnp.float32)
        made_v = jnp.dot(part, whole_v, preferred_element_type=jnp.float32)
        return (
            lax.dynamic_update_slice_in_dim(sums[0], made_k, slot * block, 0),
            lax.dynamic_update_slice_in_dim(sums[1], made_v, slot * block, 0),
        )

    fresh_k, fresh_v = lax.fori_loop(0, count_me, compute, (empty, empty))
    fresh_k = fresh_k.astype(jnp.bfloat16)
    fresh_v = fresh_v.astype(jnp.bfloat16)
    source_k = fresh_k
    source_v = fresh_v

    def write(index, caches):
        source = slot_of(index)
        target = mine_ids[index] * block
        block_k = lax.dynamic_slice_in_dim(source_k, source * block, block, 0)
        block_v = lax.dynamic_slice_in_dim(source_v, source * block, block, 0)
        return (
            lax.dynamic_update_slice_in_dim(caches[0], block_k, target, 0),
            lax.dynamic_update_slice_in_dim(caches[1], block_v, target, 0),
        )

    new_keys, new_values = lax.fori_loop(0, count_me, write, (cache_keys, cache_values))
    queries = lax.all_gather(resp_queries, "ctx", axis=0, tiled=True)
    heads_dev = width // HD
    total_rows = queries.shape[0]
    all_keys = jnp.concatenate([new_keys, resp_keys], axis=0)
    all_values = jnp.concatenate([new_values, resp_values], axis=0)
    key_count = all_keys.shape[0]
    query_heads = queries.reshape(total_rows, heads_dev, HD)
    key_heads = all_keys.reshape(key_count, heads_dev, HD)
    value_heads = all_values.reshape(key_count, heads_dev, HD)
    scores = jnp.einsum(
        "rhd,khd->hrk", query_heads, key_heads, preferred_element_type=jnp.float32
    ) * (1.0 / HD**0.5)
    group_top = jnp.max(scores, axis=2)
    weights = jnp.exp(scores - group_top[:, :, None])
    group_total = jnp.sum(weights, axis=2)
    group_mix = jnp.einsum(
        "hrk,khd->rhd",
        weights.astype(jnp.bfloat16),
        value_heads,
        preferred_element_type=jnp.float32,
    )
    top = lax.pmax(group_top, "ctx")
    factor = jnp.exp(group_top - top)
    scaled_mix = (group_mix * jnp.transpose(factor)[:, :, None]).reshape(total_rows, width)
    scaled_total = jnp.transpose(group_total * factor)
    mixed_flat, total_part = (
        lax.psum_scatter(scaled_mix, "ctx", scatter_dimension=0, tiled=True),
        lax.psum_scatter(scaled_total, "ctx", scatter_dimension=0, tiled=True),
    )
    mine_rows = mixed_flat.shape[0]
    mixed_part = mixed_flat.reshape(mine_rows, heads_dev, HD)
    attended = (mixed_part / total_part[:, :, None]).reshape(mine_rows, width)
    return (new_keys, new_values, attended.astype(jnp.bfloat16))


def solution(mesh):
    placed = (
        P("ctx", "head"),
        P(),
        P("ctx", "head"),
        P("ctx", "head"),
        P("ctx", "head"),
        P("ctx", "head"),
        P("ctx", "head"),
        P("ctx", "head"),
        P("ctx", "head"),
        P(),
        P(),
    )
    return jax.shard_map(
        body,
        mesh=mesh,
        in_specs=placed,
        out_specs=(P("ctx", "head"), P("ctx", "head"), P("ctx", "head")),
        check_vma=False,
    )
```

profile of v0, /device:TPU:1, one launch (start us, length us, event | category | flops | bytes accessed | tf_op | source)
XLA Modules:
  0.0 617.5 jit_solution(8732120649601925019)
XLA Ops:
  7.2 0.0 copy-start
  7.2 0.0 copy-start.11
  7.2 0.0 copy-start.8
  7.2 0.0 copy-start.12
  7.2 0.0 all-gather.4.cloned.1.call-start
  7.3 0.9 dynamic-slice_reduce_fusion
  8.2 0.1 broadcast_bitcast_fusion
  8.3 0.0 copy-done
  8.3 0.6 gather_fusion
  8.9 0.9 bitcast_select_fusion
  9.8 0.0 all-gather.4.cloned.1.call-update
  9.8 0.0 all-gather.6.cloned.1.call-start
  9.9 0.7 all-gather.6.cloned.1.call-update
  10.6 0.0 all-gather.8.cloned.1.call-start
  10.6 0.7 all-gather.8.cloned.1.call-update
  11.3 0.0 all-reduce.4.cloned.1.call-start
  11.4 0.0 copy-done.11
  11.4 0.6 dynamic_slice.20
  12.0 53.7 %all_gather.15 = bf16[512,512]{1,0:T(8,128)(2,1)S(1)} all-gather(bf16[8,512]{1,0:T(8,128)(2,1)S(1)} %copy-done.8), channel_id=1, replica_groups=mesh['ctx'=64,'head'=8] {'ctx'}, dimensions={0}, use_global_device_ids=true | all-gather | bytes 532480 | tf_op jit(solution)/shard_map/all_gather | solution.py:81
  65.7 0.2 copy.20
  65.9 8.5 %all-gather.4.cloned.1.call-done = bf16[512,4096]{1,0:T(8,128)(2,1)} async-done(((bf16[512,512]{1,0:T(8,128)(2,1)}), bf16[512,4096]{1,0:T(8,128)(2,1)}) %all-gather.4.cloned.1.call-update) | async-done | bytes 4194320 | tf_op jit(solution)/shard_map/all_gather | solution.py:45
  74.5 3.2 fusion.4
  77.7 0.2 copy-done.3
  77.9 3.6 fusion.6
  81.5 79.2 %all-gather.6.cloned.1.call-done = bf16[4096,512]{1,0:T(8,128)(2,1)} async-done(((bf16[64,512]{1,0:T(8,128)(2,1)}), bf16[4096,512]{1,0:T(8,128)(2,1)}) %all-gather.6.cloned.1.call-update) | async-done | bytes 4194320 | tf_op jit(solution)/shard_map/all_gather | solution.py:50
  160.7 85.3 %all-gather.8.cloned.1.call-done = bf16[4096,512]{1,0:T(8,128)(2,1)} async-done(((bf16[64,512]{1,0:T(8,128)(2,1)}), bf16[4096,512]{1,0:T(8,128)(2,1)}) %all-gather.8.cloned.1.call-update) | async-done | bytes 4194320 | tf_op jit(solution)/shard_map/all_gather | solution.py:51
  246.1 0.0 copy-start.5
  246.1 0.0 copy-start.7
  246.1 0.0 copy-start.9
  246.1 0.7 while.24
  246.9 0.3 copy-done.5
  247.1 0.2 copy-done.7
  247.3 0.7 while.25
  248.0 0.0 copy-start.6
  248.0 0.0 copy-start.4
  248.0 0.0 copy-start.10
  248.0 2.7 bitcast_reduce_fusion
  250.7 158.2 %pmax.7 = f32[4,512]{1,0:T(4,128)S(1)} all-reduce(f32[4,512]{1,0:T(4,128)S(1)} %get-tuple-element.117), channel_id=1, replica_groups=mesh['ctx'=64,'head'=8] {'ctx'}, use_global_device_ids=true, to_apply=%region_6.7 | all-reduce | flops 2048 | bytes 16384 | tf_op jit(solution)/shard_map/pmax | solution.py:102
  408.9 3.1 fusion.8
  412.0 0.4 copy-done.2
  412.3 1.0 fusion.17
  413.4 1.4 copy.24
  414.7 0.0 all-reduce.4.cloned.1.call-update
  414.8 1.3 dynamic-slice
  416.7 131.8 %all-reduce.1 = f32[512,4]{0,1:T(4,128)S(1)} all-reduce(f32[512,4]{0,1:T(4,128)S(1)} %get-tuple-element.115), channel_id=3, replica_groups=mesh['ctx'=64,'head'=8] {'ctx'}, use_global_device_ids=true, to_apply=%region_9.10.clone | all-reduce | flops 2048 | bytes 16384
  548.4 0.1 constant_dynamic-slice_fusion
  548.5 61.0 %all-reduce.4.cloned.1.call-done = f32[512,512]{1,0:T(8,128)} async-done(((f32[512,512]{1,0:T(8,128)}), f32[512,512]{1,0:T(8,128)}) %all-reduce.4.cloned.1.call-update) | async-done | bytes 1048592
  609.6 1.4 fusion.25
  (16 shorter events, 0.1 us)
Async XLA Ops:
  7.2 1.1 copy-start
  7.2 4.2 copy-start.11
  7.2 4.8 copy-start.8
  7.2 4.2 copy-start.12
  7.2 67.3 %all-gather.4.cloned.1.call-start = ((), (), s32[]{:S(2)}) async-start(), calls=%async_computation | async-start | bytes 4718592 | tf_op jit(solution)/shard_map/all_gather | solution.py:45
  9.8 150.9 %all-gather.6.cloned.1.call-start = ((), (), s32[]{:S(2)}) async-start(), calls=%async_computation.1 | async-start | bytes 4259840 | tf_op jit(solution)/shard_map/all_gather | solution.py:50
  10.6 235.4 %all-gather.8.cloned.1.call-start = ((), (), s32[]{:S(2)}) async-start(), calls=%async_computation.2 | async-start | bytes 4259840 | tf_op jit(solution)/shard_map/all_gather | solution.py:51
  11.3 598.2 %all-reduce.4.cloned.1.call-start = ((), (), s32[]{:S(2)}) async-start(), calls=%async_computation.3 | async-start | bytes 2097152
  74.5 3.4 copy-start.3
  246.1 1.1 copy-start.5
  246.1 1.2 copy-start.7
  246.1 1.9 copy-start.9
  248.0 164.0 %copy-start.6 = (bf16[512,512]{1,0:T(8,128)(2,1)}, bf16[512,512]{1,0:T(8,128)(2,1)S(1)}, u32[]{:S(2)}) copy-start(bf16[512,512]{1,0:T(8,128)(2,1)S(1)} %get-tuple-element.78) | copy-start | bytes 1572868
  248.0 164.0 %copy-start.4 = (bf16[512,512]{1,0:T(8,128)(2,1)}, bf16[512,512]{1,0:T(8,128)(2,1)S(1)}, u32[]{:S(2)}) copy-start(bf16[512,512]{1,0:T(8,128)(2,1)S(1)} %get-tuple-element.79) | copy-start | bytes 1572868
  248.0 164.0 %copy-start.10 = (bf16[8,512]{1,0:T(8,128)(2,1)S(1)}, bf16[8,512]{1,0:T(8,128)(2,1)}, u32[]{:S(2)}) copy-start(bf16[8,512]{1,0:T(8,128)(2,1)} %param.23) | copy-start | bytes 24580
  408.8 3.5 copy-start.2
Sparse Core Ops, SparseCore 0:
  10.7 63.7 all-gather.3
  77.8 82.8 all-gather.5
  164.1 81.8 all-gather.7
  414.9 194.6 all-reduce.3
where the time goes:
time: 618 us; the launch traced here: 617 us
  blocking collectives  344 us (56%)
  waiting for transfers between devices  235 us (38%)
  between operations  14.7 us (2%)
  other arithmetic  12.3 us (2%)
  local copies, waits for them, and re-layouts  6.22 us (1%)
    pmax x1, blocking collectives, body(): top = lax.pmax(group_top, 'ctx')  158 us
    unnamed x1, blocking collectives  132 us
    all_gather x1, waiting for transfers between devices, body(): lax.all_gather(value_weight, 'ctx', axis=0, tiled=True)  85.3 us
    all_gather x1, waiting for transfers between devices, body(): lax.all_gather(key_weight, 'ctx', axis=0, tiled=True)  79.2 us
    unnamed x5, waiting for transfers between devices  62.5 us
    all_gather x1, blocking collectives, body(): queries = lax.all_gather(resp_queries, 'ctx', axis=0, tiled=True)  53.7 us
  transfers between devices with their start and end apart: 4, of which 4 were waited for; matrix products, arithmetic and copies ran while one was open for 1% of the time, Pallas kernels for 0%

commit v1 on v0

v1 whole, which is shorter than its diff:
```python
import jax
import jax.numpy as jnp
from jax import lax
from jax.experimental import pallas as pl
from jax.experimental.pallas import tpu as pltpu
from jax.sharding import PartitionSpec as P

HD = 128
BLOCK = 128
NY, NX, NZ = 8, 4, 8
WROWS = 64
eps = 1e-05
LOG2E = 1.4426950408889634
F32 = jnp.float32
BF16 = jnp.bfloat16


def shift_ctx(array, dy=0, dx=0, dcore=0):
    pairs = []
    for y in range(NY):
        for x in range(NX):
            for core in range(2):
                to = (((y + dy) % NY) * NX + (x + dx) % NX) * 2 + (core ^ dcore)
                pairs.append(((y * NX + x) * 2 + core, to))
    return lax.ppermute(array, "ctx", pairs)


def put_stats(stats, lane, h, top, total):
    for first, rest in ((h * 8, top), (h * 8 + 3, total)):
        for i in range(3):
            part = rest.astype(BF16).astype(F32)
            stats = jnp.where(lane == first + i, part, stats)
            rest = rest - part
    return stats


def get_stats(stats, h):
    one = [stats[..., h * 8 + i : h * 8 + i + 1] for i in range(6)]
    return one[0] + one[1] + one[2], one[3] + one[4] + one[5]


def column_kernel(pos, *refs):
    pieces, out, held = refs[:NY], refs[NY], refs[NY + 1]
    y = pos[0]
    for a, piece in enumerate(pieces):
        row = lax.rem(y + a, NY)
        out[row] = piece[:WROWS, :]
        out[NY + row] = piece[WROWS : 2 * WROWS, :]
        held[pl.ds(pl.multiple_of(row * 8, 8), 8), :] = piece[2 * WROWS :, :].astype(F32)
    out[2 * NY] = held[...].astype(BF16)


def payload_kernel(keys, values, queries, out):
    out[:WROWS, :] = keys[...]
    out[WROWS : 2 * WROWS, :] = values[...]
    out[2 * WROWS :, :] = queries[...]


def place_from(pos):
    x, core = pos[1], pos[2]
    return lambda b, e: lax.rem(x + b, NX) * 2 + (core + e - 2 * core * e)


def project_kernel(pos, gain, xs, own, own_sw, following, last, turned, acc, pair):
    slices, rows, depth = xs.shape
    width = own.shape[2]
    pair[0] = following[...]
    pair[1] = last[...]

    def squares(j, total):
        part = xs[j].astype(F32)
        part = part * part
        return total + sum(part[:, i * 128 : (i + 1) * 128] for i in range(part.shape[1] // 128))

    summed = lax.fori_loop(0, slices, squares, jnp.zeros((rows, 128), F32))
    mean = jnp.sum(summed, axis=1, keepdims=True) * (1.0 / (slices * depth))
    scale = lax.rsqrt(mean + eps)
    low = lax.broadcasted_iota(jnp.int32, (rows, 128), 1) < WROWS
    for q in range(NX):
        cols = slice(q * 128, (q + 1) * 128)
        for u in range(slices // 2):
            one, two = (xs[j, :, cols].astype(F32) * scale * gain[j : j + 1, cols] for j in (2 * u, 2 * u + 1))
            at = slice(u * 128, (u + 1) * 128)
            turned[2 * q, :, at] = jnp.where(low, one, pltpu.roll(two, WROWS, 1)).astype(BF16)
            turned[2 * q + 1, :, at] = jnp.where(low, pltpu.roll(one, WROWS, 1), two).astype(BF16)
    place = place_from(pos)
    acc[...] = jnp.zeros_like(acc)
    for piece, b, e in ((own, 0, 0), (own_sw, 0, 1), (following, 1, 0), (last, 3, 0)):
        left = turned[place(b, e)]
        acc[:, :width] += jnp.dot(left, piece[:NY].reshape(depth, width), preferred_element_type=F32)
        acc[:, width:] += jnp.dot(left, piece[NY : 2 * NY].reshape(depth, width), preferred_element_type=F32)


def fused_kernel(*refs):
    pos, cache_k, cache_v, resp_k, resp_v, normed, acc_in = refs[:7]
    own, own_sw, pair, pair_sw, far_k, far_k_sw, far_v, far_v_sw = refs[7:15]
    new_k, new_v, packed_mine, packed_other, queries, keys, values, acc = refs[15:]
    rows, depth = normed.shape[1:]
    width = own.shape[2]
    x = pos[1]
    place = place_from(pos)

    for e, (mine, two, far) in enumerate(((own, pair, far_v), (own_sw, pair_sw, far_v_sw))):
        for b, block in enumerate((mine[2 * NY], two[0, 2 * NY], far[NY], two[1, 2 * NY])):
            queries[e * NX + lax.rem(x + b, NX)] = block
    acc[...] = acc_in[...]
    for left, of_k, of_v in (
        (place(1, 1), pair_sw[0, :NY], pair_sw[0, NY : 2 * NY]),
        (place(3, 1), pair_sw[1, :NY], pair_sw[1, NY : 2 * NY]),
        (place(2, 0), far_k[...], far_v[:NY]),
        (place(2, 1), far_k_sw[...], far_v_sw[:NY]),
    ):
        acc[:, :width] += jnp.dot(normed[left], of_k.reshape(depth, width), preferred_element_type=F32)
        acc[:, width:] += jnp.dot(normed[left], of_v.reshape(depth, width), preferred_element_type=F32)

    for b in range(rows // BLOCK):
        at = slice(b * BLOCK, (b + 1) * BLOCK)
        drifted = pos[4 + b] > 0
        keys[at, :] = jnp.where(drifted, acc[at, :width].astype(BF16), cache_k[at, :])
        values[at, :] = jnp.where(drifted, acc[at, width:].astype(BF16), cache_v[at, :])
    new_k[...] = keys[:rows, :]
    new_v[...] = values[:rows, :]
    blank = jnp.zeros((128 - resp_k.shape[0], width), F32)
    keys[rows:, :] = jnp.concatenate([resp_k[...].astype(F32), blank], axis=0).astype(BF16)
    values[rows:, :] = jnp.concatenate([resp_v[...].astype(F32), blank], axis=0).astype(BF16)
    tile = packed_mine.shape[0]
    lane = lax.broadcasted_iota(jnp.int32, (tile, 128), 1)
    score_scale = 1.0 / HD**0.5
    for t, packed in enumerate((packed_mine, packed_other)):
        query = queries[t * NX : (t + 1) * NX].reshape(tile, width)
        stats = jnp.zeros((tile, 128), F32)
        for h in range(width // HD):
            cols = slice(h * HD, (h + 1) * HD)
            scores = lax.dot_general(
                query[:, cols], keys[:, cols], (((1,), (1,)), ((), ())), preferred_element_type=F32
            )
            extra = jnp.where(lane < 8, scores[:, rows:], -jnp.inf)
            scores = scores[:, :rows]
            top = jnp.maximum(jnp.max(scores, axis=1, keepdims=True), jnp.max(extra, axis=1, keepdims=True))
            weights = jnp.exp2((scores - top) * (LOG2E * score_scale))
            extra = jnp.exp2((extra - top) * (LOG2E * score_scale))
            total = jnp.sum(weights, axis=1, keepdims=True) + jnp.sum(extra, axis=1, keepdims=True)
            weights = jnp.concatenate([weights.astype(BF16), extra.astype(BF16)], axis=1)
            packed[:, cols] = jnp.dot(weights, values[:, cols], preferred_element_type=F32).astype(BF16)
            stats = put_stats(stats, lane, h, top * score_scale, total)
        packed[:, width:] = stats.astype(BF16)


def merge_kernel(one, two, out):
    width = out.shape[1] - 128
    lane = lax.broadcasted_iota(jnp.int32, (out.shape[0], 128), 1)
    stats = [ref[:, width:].astype(F32) for ref in (one, two)]
    merged = jnp.zeros(lane.shape, F32)
    for h in range(width // HD):
        cols = slice(h * HD, (h + 1) * HD)
        (top_one, total_one), (top_two, total_two) = (get_stats(s, h) for s in stats)
        top = jnp.maximum(top_one, top_two)
        factor_one, factor_two = jnp.exp(top_one - top), jnp.exp(top_two - top)
        out[:, cols] = (one[:, cols].astype(F32) * factor_one + two[:, cols].astype(F32) * factor_two).astype(BF16)
        merged = put_stats(merged, lane, h, top, total_one * factor_one + total_two * factor_two)
    out[:, width:] = merged.astype(BF16)


def combine_kernel(parts, out):
    groups, rows = parts.shape[0] // 8, 8
    width = out.shape[1]
    stats = parts[:, width:].astype(F32).reshape(groups, rows, 128)
    for h in range(width // HD):
        cols = slice(h * HD, (h + 1) * HD)
        top, total = get_stats(stats, h)
        factor = jnp.exp(top - jnp.max(top, axis=0, keepdims=True))
        mix = parts[:, cols].astype(F32).reshape(groups, rows, HD)
        mixed = jnp.sum(mix * factor, axis=0)
        out[:, cols] = (mixed / jnp.sum(total * factor, axis=0)).astype(BF16)


def body(
    x_prompt,
    norm_gain,
    key_weight,
    value_weight,
    cache_keys,
    cache_values,
    resp_queries,
    resp_keys,
    resp_values,
    drift_ids,
    drift_count,
):
    here = lax.axis_index("ctx")
    z = lax.axis_index("head")
    y, x, core = here // (NX * 2), (here // 2) % NX, here % 2
    rows, slice_width = x_prompt.shape
    width = key_weight.shape[1]
    mine_ids = lax.dynamic_index_in_dim(drift_ids, here, 0, keepdims=False)
    count_me = lax.dynamic_index_in_dim(drift_count, here, 0, keepdims=False)
    slots = jnp.arange(drift_ids.shape[1])
    drifted = jnp.any((mine_ids[None, :] == slots[:, None]) & (slots < count_me)[None, :], axis=1)
    pos = jnp.concatenate([jnp.stack([y, x, core, z]).astype(jnp.int32), drifted.astype(jnp.int32)])

    vmem = pl.BlockSpec(memory_space=pltpu.VMEM)
    smem = pl.BlockSpec(memory_space=pltpu.SMEM)
    big = pltpu.CompilerParams(vmem_limit_bytes=30 << 20)
    x_all = lax.all_gather(x_prompt, "head", axis=0)

    payload = pl.pallas_call(
        payload_kernel,
        out_shape=jax.ShapeDtypeStruct((2 * WROWS + resp_queries.shape[0], width), BF16),
        in_specs=[vmem] * 3,
        out_specs=vmem,
        compiler_params=pltpu.CompilerParams(vmem_limit_bytes=16 << 20),
        name="payload",
    )(key_weight, value_weight, resp_queries)
    near = {a: shift_ctx(payload, dy=-a) for a in (3, 5, 2, 6, 1, 7)}
    near[4] = shift_ctx(near[5], dy=1)
    column = pl.pallas_call(
        column_kernel,
        out_shape=jax.ShapeDtypeStruct((2 * NY + 1, WROWS, width), BF16),
        in_specs=[smem] + [vmem] * NY,
        out_specs=vmem,
        scratch_shapes=[pltpu.VMEM((NY * resp_queries.shape[0], width), F32)],
        compiler_params=pltpu.CompilerParams(vmem_limit_bytes=16 << 20),
        name="column",
    )(pos, payload, *[near[a] for a in range(1, NY)])
    following, last = shift_ctx(column, dx=-1), shift_ctx(column, dx=1)
    far_k, far_v = shift_ctx(last[:NY], dx=1), shift_ctx(following[NY:], dx=-1)
    own_sw = shift_ctx(column, dcore=1)
    normed, partial, pair = pl.pallas_call(
        project_kernel,
        out_shape=(
            jax.ShapeDtypeStruct((NZ, rows, slice_width), BF16),
            jax.ShapeDtypeStruct((rows, 2 * width), F32),
            jax.ShapeDtypeStruct((2,) + column.shape, BF16),
        ),
        in_specs=[smem] + [vmem] * 6,
        out_specs=(vmem, vmem, vmem),
        compiler_params=big,
        cost_estimate=pl.CostEstimate(flops=3 << 30, bytes_accessed=24 << 20, transcendentals=512),
        name="norm_project",
    )(pos, norm_gain.astype(F32).reshape(NZ, slice_width), x_all, column, own_sw, following, last)
    pair_sw = shift_ctx(lax.optimization_barrier((pair, far_k, far_v))[0], dcore=1)
    far_k_sw, far_v_sw = shift_ctx(far_k, dcore=1), shift_ctx(far_v, dcore=1)

    total = 2 * NY * NX * resp_queries.shape[0]
    result = jax.ShapeDtypeStruct((total // 2, width + 128), BF16)
    new_keys, new_values, packed_mine, packed_other = pl.pallas_call(
        fused_kernel,
        out_shape=(
            jax.ShapeDtypeStruct((rows, width), BF16),
            jax.ShapeDtypeStruct((rows, width), BF16),
            result,
            result,
        ),
        in_specs=[smem] + [vmem] * 14,
        out_specs=(vmem, vmem, vmem, vmem),
        scratch_shapes=[
            pltpu.VMEM((2 * NX, WROWS, width), BF16),
            pltpu.VMEM((rows + 128, width), BF16),
            pltpu.VMEM((rows + 128, width), BF16),
            pltpu.VMEM((rows, 2 * width), F32),
        ],
        compiler_params=big,
        cost_estimate=pl.CostEstimate(flops=3 << 30, bytes_accessed=12 << 20, transcendentals=1 << 20),
        name="refresh_attend",
    )(
        pos,
        cache_keys,
        cache_values,
        resp_keys,
        resp_values,
        normed,
        partial,
        column,
        own_sw,
        pair,
        pair_sw,
        far_k,
        far_k_sw,
        far_v,
        far_v_sw,
    )
    merged = pl.pallas_call(
        merge_kernel,
        out_shape=result,
        in_specs=[vmem, vmem],
        out_specs=vmem,
        compiler_params=pltpu.CompilerParams(vmem_limit_bytes=16 << 20),
        name="merge",
    )(packed_mine, shift_ctx(packed_other, dcore=1))
    same = [[(j * NX + i) * 2 + c for i in range(NX) for j in range(NY)] for c in range(2)]
    parts = lax.all_to_all(merged, "ctx", 0, 0, axis_index_groups=same, tiled=True)
    attended = pl.pallas_call(
        combine_kernel,
        out_shape=jax.ShapeDtypeStruct((resp_queries.shape[0], width), BF16),
        in_specs=[vmem],
        out_specs=vmem,
        compiler_params=pltpu.CompilerParams(vmem_limit_bytes=16 << 20),
        name="combine",
    )(parts)
    return new_keys, new_values, attended


def solution(mesh):
    placed = (
        P("ctx", "head"),
        P(),
        P("ctx", "head"),
        P("ctx", "head"),
        P("ctx", "head"),
        P("ctx", "head"),
        P("ctx", "head"),
        P("ctx", "head"),
        P("ctx", "head"),
        P(),
        P(),
    )
    return jax.shard_map(
        body,
        mesh=mesh,
        in_specs=placed,
        out_specs=(P("ctx", "head"), P("ctx", "head"), P("ctx", "head")),
        check_vma=False,
    )
```

time: 618 us -> 143 us (0.23)
  the two profiles are of different devices: /device:TPU:1 before, /device:TPU:392 now
where the time goes in v1:
time: 143 us; the launch traced here: 142 us
  starting transfers between devices  50.4 us (35%)
  waiting for transfers between devices  29.7 us (21%)
  blocking collectives  19.8 us (14%)
  Pallas kernels  16 us (11%)
  between operations  14.4 us (10%)
  local copies, waits for them, and re-layouts  11.4 us (8%)
    ppermute x16, starting transfers between devices, shift_ctx(): return lax.ppermute(array, 'ctx', pairs)  50.4 us
    ppermute x16, waiting for transfers between devices, shift_ctx(): return lax.ppermute(array, 'ctx', pairs)  29 us
    all_to_all x1, blocking collectives, body(): lax.all_to_all(merged, 'ctx', 0, 0, axis_index_groups=same, tiled=True)  19.8 us
    unnamed x28, local copies, waits for them, and re-layouts  8.09 us
    pallas_call x1, Pallas kernels, body(): pl.pallas_call(project_kernel, out_shape=(jax.ShapeDtypeStruct((NZ, rows,...  6.74 us
    pallas_call x1, Pallas kernels, body(): pl.pallas_call(fused_kernel, out_shape=(jax.ShapeDtypeStruct((rows, width...  6.4 us
  transfers between devices with their start and end apart: 17, of which 8 were waited for; matrix products, arithmetic and copies ran while one was open for 3% of the time, Pallas kernels for 5%

profile of v1, /device:TPU:392, one launch (start us, length us, event | category | flops | bytes accessed | tf_op | source)
XLA Modules:
  0.0 142.4 jit_solution(5308768093144635821)
XLA Ops:
  7.2 0.0 copy-start
  7.2 0.0 all-gather.3.cloned.1.call-start
  7.2 0.7 all-gather.3.cloned.1.call-update
  7.9 0.8 copy-done.7
  8.8 0.8 copy-done.8
  9.6 0.7 copy-done.11
  10.3 6.7 %collective-permute-start.3 = (bf16[136,512]{1,0:T(8,128)(2,1)S(1)}, bf16[136,512]{1,0:T(8,128)(2,1)S(1)}, u32[]{:S(2)}, u32[]{:S(2)}) collective-permute-start(bf16[136,512]{1,0:T(8,128)(2,1)S(1)} %payload.1.refs_0_), channel_id=1, source_target_pairs={{0,192},{8,200},{16,208},{24,216},{32,224},{40,232},{48,240},{56,2... | collective-permute-start | bytes 417800 | tf_op jit(solution)/shard_map/ppermute | solution.py:25
  17.0 1.9 %collective-permute-start = (bf16[136,512]{1,0:T(8,128)(2,1)S(1)}, bf16[136,512]{1,0:T(8,128)(2,1)S(1)}, u32[]{:S(2)}, u32[]{:S(2)}) collective-permute-start(bf16[136,512]{1,0:T(8,128)(2,1)S(1)} %payload.1.refs_0_), channel_id=1, source_target_pairs={{0,448},{8,456},{16,464},{24,472},{32,480},{40,488},{48,496},{56,5... | collective-permute-start | bytes 417800 | tf_op jit(solution)/shard_map/ppermute | solution.py:25
  19.0 2.7 %collective-permute-start.1 = (bf16[136,512]{1,0:T(8,128)(2,1)S(1)}, bf16[136,512]{1,0:T(8,128)(2,1)S(1)}, u32[]{:S(2)}, u32[]{:S(2)}) collective-permute-start(bf16[136,512]{1,0:T(8,128)(2,1)S(1)} %payload.1.refs_0_), channel_id=1, source_target_pairs={{0,384},{8,392},{16,400},{24,408},{32,416},{40,424},{48,432},{56,4... | collective-permute-start | bytes 417800 | tf_op jit(solution)/shard_map/ppermute | solution.py:25
  21.7 6.0 %collective-permute-start.2 = (bf16[136,512]{1,0:T(8,128)(2,1)S(1)}, bf16[136,512]{1,0:T(8,128)(2,1)S(1)}, u32[]{:S(2)}, u32[]{:S(2)}) collective-permute-start(bf16[136,512]{1,0:T(8,128)(2,1)S(1)} %payload.1.refs_0_), channel_id=1, source_target_pairs={{0,320},{8,328},{16,336},{24,344},{32,352},{40,360},{48,368},{56,3... | collective-permute-start | bytes 417800 | tf_op jit(solution)/shard_map/ppermute | solution.py:25
  27.7 1.9 %collective-permute-start.5 = (bf16[136,512]{1,0:T(8,128)(2,1)S(1)}, bf16[136,512]{1,0:T(8,128)(2,1)S(1)}, u32[]{:S(2)}, u32[]{:S(2)}) collective-permute-start(bf16[136,512]{1,0:T(8,128)(2,1)S(1)} %payload.1.refs_0_), channel_id=1, source_target_pairs={{0,128},{8,136},{16,144},{24,152},{32,160},{40,168},{48,176},{56,1... | collective-permute-start | bytes 417800 | tf_op jit(solution)/shard_map/ppermute | solution.py:25
  29.6 1.2 dynamic_slice.9
  30.9 3.3 %collective-permute-start.6 = (bf16[136,512]{1,0:T(8,128)(2,1)S(1)}, bf16[136,512]{1,0:T(8,128)(2,1)S(1)}, u32[]{:S(2)}, u32[]{:S(2)}) collective-permute-start(bf16[136,512]{1,0:T(8,128)(2,1)S(1)} %payload.1.refs_0_), channel_id=1, source_target_pairs={{0,64},{8,72},{16,80},{24,88},{32,96},{40,104},{48,112},{56,120},{... | collective-permute-start | bytes 417800 | tf_op jit(solution)/shard_map/ppermute | solution.py:25
  34.3 3.5 %collective-permute-start.4 = (bf16[136,512]{1,0:T(8,128)(2,1)S(1)}, bf16[136,512]{1,0:T(8,128)(2,1)S(1)}, u32[]{:S(2)}, u32[]{:S(2)}) collective-permute-start(bf16[136,512]{1,0:T(8,128)(2,1)S(1)} %collective-permute-done.3.refs_5_), channel_id=1, source_target_pairs={{0,64},{8,72},{16,80},{24,88},{32,96},{40,104},{48,112},{56,120},{... | collective-permute-start | bytes 417800 | tf_op jit(solution)/shard_map/ppermute | solution.py:25
  37.7 0.7 iota_compare_fusion.1
  38.5 0.2 dynamic-slice_reduce_fusion
  38.6 0.1 fusion.1
  38.8 0.1 concatenate.3.pos.refs_0_
  38.9 0.7 collective-permute-done.2.refs_3_
  39.6 0.6 collective-permute-done.5.refs_6_
  40.2 0.5 collective-permute-done.6.refs_7_
  40.7 2.2 %collective-permute-done.4.refs_4_ = bf16[136,512]{1,0:T(8,128)(2,1)S(1)} collective-permute-done((bf16[136,512]{1,0:T(8,128)(2,1)S(1)}, bf16[136,512]{1,0:T(8,128)(2,1)S(1)}, u32[]{:S(2)}, u32[]{:S(2)}) %collective-permute-start.4) | collective-permute-done | bytes 139296 | tf_op jit(solution)/shard_map/ppermute | solution.py:25
  42.9 0.6 column.1.own.refs_7_
  43.6 4.7 %collective-permute-start.8 = (bf16[17,64,512]{2,1,0:T(8,128)(2,1)S(1)}, bf16[17,64,512]{2,1,0:T(8,128)(2,1)S(1)}, u32[]{:S(2)}, u32[]{:S(2)}) collective-permute-start(bf16[17,64,512]{2,1,0:T(8,128)(2,1)S(1)} %column.1.own.refs_7_), channel_id=1, source_target_pairs={{0,48},{8,56},{16,0},{24,8},{32,16},{40,24},{48,32},{56,40},{64,11... | collective-permute-start | bytes 3342344 | tf_op jit(solution)/shard_map/ppermute | solution.py:25
  48.3 1.9 %collective-permute-start.9 = (bf16[17,64,512]{2,1,0:T(8,128)(2,1)S(1)}, bf16[17,64,512]{2,1,0:T(8,128)(2,1)S(1)}, u32[]{:S(2)}, u32[]{:S(2)}) collective-permute-start(bf16[17,64,512]{2,1,0:T(8,128)(2,1)S(1)} %column.1.own.refs_7_), channel_id=1, source_target_pairs={{0,16},{8,24},{16,32},{24,40},{32,48},{40,56},{48,0},{56,8},{64,80... | collective-permute-start | bytes 3342344 | tf_op jit(solution)/shard_map/ppermute | solution.py:25
  50.2 1.9 %collective-permute-start.7 = (bf16[17,64,512]{2,1,0:T(8,128)(2,1)S(1)}, bf16[17,64,512]{2,1,0:T(8,128)(2,1)S(1)}, u32[]{:S(2)}, u32[]{:S(2)}) collective-permute-start(bf16[17,64,512]{2,1,0:T(8,128)(2,1)S(1)} %column.1.own.refs_7_), channel_id=1, source_target_pairs={{0,8},{8,0},{16,24},{24,16},{32,40},{40,32},{48,56},{56,48},{64,72... | collective-permute-start | bytes 3342344 | tf_op jit(solution)/shard_map/ppermute | solution.py:25
  52.1 19.6 %collective-permute-done.8.following = bf16[17,64,512]{2,1,0:T(8,128)(2,1)S(1)} collective-permute-done((bf16[17,64,512]{2,1,0:T(8,128)(2,1)S(1)}, bf16[17,64,512]{2,1,0:T(8,128)(2,1)S(1)}, u32[]{:S(2)}, u32[]{:S(2)}) %collective-permute-start.8) | collective-permute-done | bytes 1114144 | tf_op jit(solution)/shard_map/ppermute | solution.py:25
  71.7 0.9 slice.9
  72.6 5.6 %collective-permute-start.11 = (bf16[9,64,512]{2,1,0:T(8,128)(2,1)}, bf16[9,64,512]{2,1,0:T(8,128)(2,1)S(1)}, u32[]{:S(2)}, u32[]{:S(2)}) collective-permute-start(bf16[9,64,512]{2,1,0:T(8,128)(2,1)} %slice.9), channel_id=1, source_target_pairs={{0,48},{8,56},{16,0},{24,8},{32,16},{40,24},{48,32},{56,40},{64,11... | collective-permute-start | bytes 1769480 | tf_op jit(solution)/shard_map/ppermute | solution.py:25
  78.2 0.8 slice.8
  79.1 1.0 copy-done.5
  80.1 1.9 %collective-permute-start.10 = (bf16[8,64,512]{2,1,0:T(8,128)(2,1)}, bf16[8,64,512]{2,1,0:T(8,128)(2,1)S(1)}, u32[]{:S(2)}, u32[]{:S(2)}) collective-permute-start(bf16[8,64,512]{2,1,0:T(8,128)(2,1)} %slice.8), channel_id=1, source_target_pairs={{0,16},{8,24},{16,32},{24,40},{32,48},{40,56},{48,0},{56,8},{64,80... | collective-permute-start | bytes 1572872 | tf_op jit(solution)/shard_map/ppermute | solution.py:25
  82.0 0.0 all-gather.3.cloned.1.call-done
  82.1 1.2 copy-done.4
  83.3 1.2 copy-done.6
  84.6 2.2 %copy-done.12 = bf16[4096,512]{1,0:T(8,128)(2,1)S(1)} copy-done((bf16[4096,512]{1,0:T(8,128)(2,1)S(1)}, bf16[4096,512]{1,0:T(8,128)(2,1)}, u32[]{:S(2)}) %copy-start.12) | copy-done | bytes 4194328
  86.8 6.7 %norm_project.1 = (bf16[8,512,512]{2,1,0:T(8,128)(2,1)S(1)}, f32[512,1024]{1,0:T(8,128)S(1)}, bf16[2,17,64,512]{3,2,1,0:T(8,128)(2,1)S(1)}) custom-call(s32[8]{0:T(128)S(1)} %concatenate.3.pos.refs_0_, f32[8,512]{1,0:T(8,128)S(1)} %reshape.20.gain, bf16[8,512,512]{2,1,0:T(8,128)(2,1)S(1)} %bitcast.10, bf16[17,64,512]{2,1,0:T(8,128)(2,1)S(1)} %column.1.own.refs_7_, ...), custom_call_target="tpu_custom_call" | custom-call | flops 3221225472 | bytes 25165824 | tf_op jit(solution)/shard_map/norm_project/pallas_call | solution.py:228
  93.5 2.0 %collective-permute-done.10.refs_11_ = bf16[8,64,512]{2,1,0:T(8,128)(2,1)S(1)} collective-permute-done((bf16[8,64,512]{2,1,0:T(8,128)(2,1)}, bf16[8,64,512]{2,1,0:T(8,128)(2,1)S(1)}, u32[]{:S(2)}, u32[]{:S(2)}) %collective-permute-start.10) | collective-permute-done | bytes 524320 | tf_op jit(solution)/shard_map/ppermute | solution.py:25
  95.5 1.9 %collective-permute-start.12 = (bf16[2,17,64,512]{3,2,1,0:T(8,128)(2,1)S(1)}, bf16[2,17,64,512]{3,2,1,0:T(8,128)(2,1)S(1)}, u32[]{:S(2)}, u32[]{:S(2)}) collective-permute-start(bf16[2,17,64,512]{3,2,1,0:T(8,128)(2,1)S(1)} %get-tuple-element.14.refs_9_), channel_id=1, source_target_pairs={{0,8},{8,0},{16,24},{24,16},{32,40},{40,32},{48,56},{56,48},{64,72... | collective-permute-start | bytes 6684680 | tf_op jit(solution)/shard_map/ppermute | solution.py:25
  97.4 2.4 %collective-permute-start.14 = (bf16[9,64,512]{2,1,0:T(8,128)(2,1)S(1)}, bf16[9,64,512]{2,1,0:T(8,128)(2,1)S(1)}, u32[]{:S(2)}, u32[]{:S(2)}) collective-permute-start(bf16[9,64,512]{2,1,0:T(8,128)(2,1)S(1)} %collective-permute-done.11.refs_13_), channel_id=1, source_target_pairs={{0,8},{8,0},{16,24},{24,16},{32,40},{40,32},{48,56},{56,48},{64,72... | collective-permute-start | bytes 1769480 | tf_op jit(solution)/shard_map/ppermute | solution.py:25
  99.8 1.9 %collective-permute-start.13 = (bf16[8,64,512]{2,1,0:T(8,128)(2,1)S(1)}, bf16[8,64,512]{2,1,0:T(8,128)(2,1)S(1)}, u32[]{:S(2)}, u32[]{:S(2)}) collective-permute-start(bf16[8,64,512]{2,1,0:T(8,128)(2,1)S(1)} %collective-permute-done.10.refs_11_), channel_id=1, source_target_pairs={{0,8},{8,0},{16,24},{24,16},{32,40},{40,32},{48,56},{56,48},{64,72... | collective-permute-start | bytes 1572872 | tf_op jit(solution)/shard_map/ppermute | solution.py:25
  101.7 1.9 %collective-permute-done.13.refs_12_ = bf16[8,64,512]{2,1,0:T(8,128)(2,1)S(1)} collective-permute-done((bf16[8,64,512]{2,1,0:T(8,128)(2,1)S(1)}, bf16[8,64,512]{2,1,0:T(8,128)(2,1)S(1)}, u32[]{:S(2)}, u32[]{:S(2)}) %collective-permute-start.13) | collective-permute-done | bytes 524320 | tf_op jit(solution)/shard_map/ppermute | solution.py:25
  103.7 6.4 %refresh_attend.1 = (bf16[512,512]{1,0:T(8,128)(2,1)}, bf16[512,512]{1,0:T(8,128)(2,1)}, bf16[256,640]{1,0:T(8,128)(2,1)S(1)}, bf16[256,640]{1,0:T(8,128)(2,1)S(1)}) custom-call(s32[8]{0:T(128)S(1)} %concatenate.3.pos.refs_0_, bf16[512,512]{1,0:T(8,128)(2,1)S(1)} %copy-done.1, bf16[512,512]{1,0:T(8,128)(2,1)S(1)} %copy-done.2, bf16[8,512]{1,0:T(8,128)(2,1)S(1)} %copy-done.9, ...), custom_call_target="tpu_custom_call" | custom-call | flops 3221225472 | bytes 12582912 | tf_op jit(solution)/shard_map/refresh_attend/pallas_call | solution.py:246
  110.1 2.0 %collective-permute-start.15 = (bf16[256,640]{1,0:T(8,128)(2,1)S(1)}, bf16[256,640]{1,0:T(8,128)(2,1)S(1)}, u32[]{:S(2)}, u32[]{:S(2)}) collective-permute-start(bf16[256,640]{1,0:T(8,128)(2,1)S(1)} %get-tuple-element.18), channel_id=1, source_target_pairs={{0,8},{8,0},{16,24},{24,16},{32,40},{40,32},{48,56},{56,48},{64,72... | collective-permute-start | bytes 983048 | tf_op jit(solution)/shard_map/ppermute | solution.py:25
  112.1 1.5 %collective-permute-done.15.two = bf16[256,640]{1,0:T(8,128)(2,1)S(1)} collective-permute-done((bf16[256,640]{1,0:T(8,128)(2,1)S(1)}, bf16[256,640]{1,0:T(8,128)(2,1)S(1)}, u32[]{:S(2)}, u32[]{:S(2)}) %collective-permute-start.15) | collective-permute-done | bytes 327712 | tf_op jit(solution)/shard_map/ppermute | solution.py:25
  113.6 1.0 merge.1
  114.6 19.8 %all_to_all.11 = bf16[32,8,640]{2,1,0:T(8,128)(2,1)S(1)} all-to-all(bf16[32,8,640]{2,1,0:T(8,128)(2,1)S(1)} %bitcast.9), channel_id=1, replica_groups={{0,64,128,192,256,320,384,448,16,80,144,208,272,336,400,464,32,96,160,2..., dimensions={0} | all-to-all | bytes 655360 | tf_op jit(solution)/shard_map/all_to_all | solution.py:291
  134.4 1.2 combine.1
  (31 shorter events, 0.1 us)
Async XLA Ops:
  7.2 31.3 %copy-start = (s32[64,4]{0,1:T(4,128)S(1)}, s32[64,4]{0,1:T(4,128)}, u32[]{:S(2)}) copy-start(s32[64,4]{0,1:T(4,128)} %param.20) | copy-start | bytes 3076
  7.2 74.9 %all-gather.3.cloned.1.call-start = ((), (), s32[]{:S(2)}) async-start(), calls=%async_computation.1 | async-start | bytes 4718592 | tf_op jit(solution)/shard_map/all_gather | solution.py:204
  7.9 0.8 copy-start.7
  8.8 0.8 copy-start.8
  9.6 0.7 copy-start.11
  10.3 20.6 %collective-permute-start.3 = (bf16[136,512]{1,0:T(8,128)(2,1)S(1)}, bf16[136,512]{1,0:T(8,128)(2,1)S(1)}, u32[]{:S(2)}, u32[]{:S(2)}) collective-permute-start(bf16[136,512]{1,0:T(8,128)(2,1)S(1)} %payload.1.refs_0_), channel_id=1, source_target_pairs={{0,192},{8,200},{16,208},{24,216},{32,224},{40,232},{48,240},{56,2... | collective-permute-start | bytes 417800 | tf_op jit(solution)/shard_map/ppermute | solution.py:25
  17.0 17.2 %collective-permute-start = (bf16[136,512]{1,0:T(8,128)(2,1)S(1)}, bf16[136,512]{1,0:T(8,128)(2,1)S(1)}, u32[]{:S(2)}, u32[]{:S(2)}) collective-permute-start(bf16[136,512]{1,0:T(8,128)(2,1)S(1)} %payload.1.refs_0_), channel_id=1, source_target_pairs={{0,448},{8,456},{16,464},{24,472},{32,480},{40,488},{48,496},{56,5... | collective-permute-start | bytes 417800 | tf_op jit(solution)/shard_map/ppermute | solution.py:25
  19.0 19.9 %collective-permute-start.1 = (bf16[136,512]{1,0:T(8,128)(2,1)S(1)}, bf16[136,512]{1,0:T(8,128)(2,1)S(1)}, u32[]{:S(2)}, u32[]{:S(2)}) collective-permute-start(bf16[136,512]{1,0:T(8,128)(2,1)S(1)} %payload.1.refs_0_), channel_id=1, source_target_pairs={{0,384},{8,392},{16,400},{24,408},{32,416},{40,424},{48,432},{56,4... | collective-permute-start | bytes 417800 | tf_op jit(solution)/shard_map/ppermute | solution.py:25
  21.7 18.0 %collective-permute-start.2 = (bf16[136,512]{1,0:T(8,128)(2,1)S(1)}, bf16[136,512]{1,0:T(8,128)(2,1)S(1)}, u32[]{:S(2)}, u32[]{:S(2)}) collective-permute-start(bf16[136,512]{1,0:T(8,128)(2,1)S(1)} %payload.1.refs_0_), channel_id=1, source_target_pairs={{0,320},{8,328},{16,336},{24,344},{32,352},{40,360},{48,368},{56,3... | collective-permute-start | bytes 417800 | tf_op jit(solution)/shard_map/ppermute | solution.py:25
  27.7 12.5 %collective-permute-start.5 = (bf16[136,512]{1,0:T(8,128)(2,1)S(1)}, bf16[136,512]{1,0:T(8,128)(2,1)S(1)}, u32[]{:S(2)}, u32[]{:S(2)}) collective-permute-start(bf16[136,512]{1,0:T(8,128)(2,1)S(1)} %payload.1.refs_0_), channel_id=1, source_target_pairs={{0,128},{8,136},{16,144},{24,152},{32,160},{40,168},{48,176},{56,1... | collective-permute-start | bytes 417800 | tf_op jit(solution)/shard_map/ppermute | solution.py:25
  30.9 9.8 %collective-permute-start.6 = (bf16[136,512]{1,0:T(8,128)(2,1)S(1)}, bf16[136,512]{1,0:T(8,128)(2,1)S(1)}, u32[]{:S(2)}, u32[]{:S(2)}) collective-permute-start(bf16[136,512]{1,0:T(8,128)(2,1)S(1)} %payload.1.refs_0_), channel_id=1, source_target_pairs={{0,64},{8,72},{16,80},{24,88},{32,96},{40,104},{48,112},{56,120},{... | collective-permute-start | bytes 417800 | tf_op jit(solution)/shard_map/ppermute | solution.py:25
  34.3 8.7 %collective-permute-start.4 = (bf16[136,512]{1,0:T(8,128)(2,1)S(1)}, bf16[136,512]{1,0:T(8,128)(2,1)S(1)}, u32[]{:S(2)}, u32[]{:S(2)}) collective-permute-start(bf16[136,512]{1,0:T(8,128)(2,1)S(1)} %collective-permute-done.3.refs_5_), channel_id=1, source_target_pairs={{0,64},{8,72},{16,80},{24,88},{32,96},{40,104},{48,112},{56,120},{... | collective-permute-start | bytes 417800 | tf_op jit(solution)/shard_map/ppermute | solution.py:25
  38.9 43.1 %copy-start.13 = (bf16[4096]{0:T(1024)(128)(2,1)S(1)}, bf16[4096]{0:T(1024)(128)(2,1)}, u32[]{:S(2)}) copy-start(bf16[4096]{0:T(1024)(128)(2,1)} %param.12) | copy-start | bytes 24580
  43.6 28.1 %collective-permute-start.8 = (bf16[17,64,512]{2,1,0:T(8,128)(2,1)S(1)}, bf16[17,64,512]{2,1,0:T(8,128)(2,1)S(1)}, u32[]{:S(2)}, u32[]{:S(2)}) collective-permute-start(bf16[17,64,512]{2,1,0:T(8,128)(2,1)S(1)} %column.1.own.refs_7_), channel_id=1, source_target_pairs={{0,48},{8,56},{16,0},{24,8},{32,16},{40,24},{48,32},{56,40},{64,11... | collective-permute-start | bytes 3342344 | tf_op jit(solution)/shard_map/ppermute | solution.py:25
  48.3 29.9 %collective-permute-start.9 = (bf16[17,64,512]{2,1,0:T(8,128)(2,1)S(1)}, bf16[17,64,512]{2,1,0:T(8,128)(2,1)S(1)}, u32[]{:S(2)}, u32[]{:S(2)}) collective-permute-start(bf16[17,64,512]{2,1,0:T(8,128)(2,1)S(1)} %column.1.own.refs_7_), channel_id=1, source_target_pairs={{0,16},{8,24},{16,32},{24,40},{32,48},{40,56},{48,0},{56,8},{64,80... | collective-permute-start | bytes 3342344 | tf_op jit(solution)/shard_map/ppermute | solution.py:25
  50.2 31.8 %collective-permute-start.7 = (bf16[17,64,512]{2,1,0:T(8,128)(2,1)S(1)}, bf16[17,64,512]{2,1,0:T(8,128)(2,1)S(1)}, u32[]{:S(2)}, u32[]{:S(2)}) collective-permute-start(bf16[17,64,512]{2,1,0:T(8,128)(2,1)S(1)} %column.1.own.refs_7_), channel_id=1, source_target_pairs={{0,8},{8,0},{16,24},{24,16},{32,40},{40,32},{48,56},{56,48},{64,72... | collective-permute-start | bytes 3342344 | tf_op jit(solution)/shard_map/ppermute | solution.py:25
  71.7 6.5 %copy-start.3 = (bf16[17,64,512]{2,1,0:T(8,128)(2,1)}, bf16[17,64,512]{2,1,0:T(8,128)(2,1)S(1)}, u32[]{:S(2)}) copy-start(bf16[17,64,512]{2,1,0:T(8,128)(2,1)S(1)} %collective-permute-done.8.following) | copy-start | bytes 3342340
  72.6 22.9 %collective-permute-start.11 = (bf16[9,64,512]{2,1,0:T(8,128)(2,1)}, bf16[9,64,512]{2,1,0:T(8,128)(2,1)S(1)}, u32[]{:S(2)}, u32[]{:S(2)}) collective-permute-start(bf16[9,64,512]{2,1,0:T(8,128)(2,1)} %slice.9), channel_id=1, source_target_pairs={{0,48},{8,56},{16,0},{24,8},{32,16},{40,24},{48,32},{56,40},{64,11... | collective-permute-start | bytes 1769480 | tf_op jit(solution)/shard_map/ppermute | solution.py:25
  79.1 1.0 copy-start.5
  80.1 15.4 %collective-permute-start.10 = (bf16[8,64,512]{2,1,0:T(8,128)(2,1)}, bf16[8,64,512]{2,1,0:T(8,128)(2,1)S(1)}, u32[]{:S(2)}, u32[]{:S(2)}) collective-permute-start(bf16[8,64,512]{2,1,0:T(8,128)(2,1)} %slice.8), channel_id=1, source_target_pairs={{0,16},{8,24},{16,32},{24,40},{32,48},{40,56},{48,0},{56,8},{64,80... | collective-permute-start | bytes 1572872 | tf_op jit(solution)/shard_map/ppermute | solution.py:25
  82.1 1.2 copy-start.4
  83.3 1.2 copy-start.6
  84.6 2.2 %copy-start.12 = (bf16[4096,512]{1,0:T(8,128)(2,1)S(1)}, bf16[4096,512]{1,0:T(8,128)(2,1)}, u32[]{:S(2)}) copy-start(bf16[4096,512]{1,0:T(8,128)(2,1)} %all-gather.3.cloned.1.call-done) | copy-start | bytes 12582916
  86.7 16.9 %copy-start.1 = (bf16[512,512]{1,0:T(8,128)(2,1)S(1)}, bf16[512,512]{1,0:T(8,128)(2,1)}, u32[]{:S(2)}) copy-start(bf16[512,512]{1,0:T(8,128)(2,1)} %refs_1_.1) | copy-start | bytes 1572868
  86.8 16.9 %copy-start.2 = (bf16[512,512]{1,0:T(8,128)(2,1)S(1)}, bf16[512,512]{1,0:T(8,128)(2,1)}, u32[]{:S(2)}) copy-start(bf16[512,512]{1,0:T(8,128)(2,1)} %refs_2_.1) | copy-start | bytes 1572868
  86.8 16.9 %copy-start.9 = (bf16[8,512]{1,0:T(8,128)(2,1)S(1)}, bf16[8,512]{1,0:T(8,128)(2,1)}, u32[]{:S(2)}) copy-start(bf16[8,512]{1,0:T(8,128)(2,1)} %refs_3_.1) | copy-start | bytes 24580
  86.8 16.9 %copy-start.10 = (bf16[8,512]{1,0:T(8,128)(2,1)S(1)}, bf16[8,512]{1,0:T(8,128)(2,1)}, u32[]{:S(2)}) copy-start(bf16[8,512]{1,0:T(8,128)(2,1)} %refs_4_.1) | copy-start | bytes 24580
  95.5 8.1 %collective-permute-start.12 = (bf16[2,17,64,512]{3,2,1,0:T(8,128)(2,1)S(1)}, bf16[2,17,64,512]{3,2,1,0:T(8,128)(2,1)S(1)}, u32[]{:S(2)}, u32[]{:S(2)}) collective-permute-start(bf16[2,17,64,512]{3,2,1,0:T(8,128)(2,1)S(1)} %get-tuple-element.14.refs_9_), channel_id=1, source_target_pairs={{0,8},{8,0},{16,24},{24,16},{32,40},{40,32},{48,56},{56,48},{64,72... | collective-permute-start | bytes 6684680 | tf_op jit(solution)/shard_map/ppermute | solution.py:25
  97.4 6.2 %collective-permute-start.14 = (bf16[9,64,512]{2,1,0:T(8,128)(2,1)S(1)}, bf16[9,64,512]{2,1,0:T(8,128)(2,1)S(1)}, u32[]{:S(2)}, u32[]{:S(2)}) collective-permute-start(bf16[9,64,512]{2,1,0:T(8,128)(2,1)S(1)} %collective-permute-done.11.refs_13_), channel_id=1, source_target_pairs={{0,8},{8,0},{16,24},{24,16},{32,40},{40,32},{48,56},{56,48},{64,72... | collective-permute-start | bytes 1769480 | tf_op jit(solution)/shard_map/ppermute | solution.py:25
  99.8 3.8 %collective-permute-start.13 = (bf16[8,64,512]{2,1,0:T(8,128)(2,1)S(1)}, bf16[8,64,512]{2,1,0:T(8,128)(2,1)S(1)}, u32[]{:S(2)}, u32[]{:S(2)}) collective-permute-start(bf16[8,64,512]{2,1,0:T(8,128)(2,1)S(1)} %collective-permute-done.10.refs_11_), channel_id=1, source_target_pairs={{0,8},{8,0},{16,24},{24,16},{32,40},{40,32},{48,56},{56,48},{64,72... | collective-permute-start | bytes 1572872 | tf_op jit(solution)/shard_map/ppermute | solution.py:25
  110.1 3.5 %collective-permute-start.15 = (bf16[256,640]{1,0:T(8,128)(2,1)S(1)}, bf16[256,640]{1,0:T(8,128)(2,1)S(1)}, u32[]{:S(2)}, u32[]{:S(2)}) collective-permute-start(bf16[256,640]{1,0:T(8,128)(2,1)S(1)} %get-tuple-element.18), channel_id=1, source_target_pairs={{0,8},{8,0},{16,24},{24,16},{32,40},{40,32},{48,56},{56,48},{64,72... | collective-permute-start | bytes 983048 | tf_op jit(solution)/shard_map/ppermute | solution.py:25
Sparse Core Ops, SparseCore 0:
  10.1 55.7 all-gather.2

commit v2 on v1

--- a/solution.py
+++ b/solution.py
@@ -200,7 +200,7 @@
 
     vmem = pl.BlockSpec(memory_space=pltpu.VMEM)
     smem = pl.BlockSpec(memory_space=pltpu.SMEM)
-    big = pltpu.CompilerParams(vmem_limit_bytes=30 << 20)
+    big = pltpu.CompilerParams(vmem_limit_bytes=16 << 20)
     x_all = lax.all_gather(x_prompt, "head", axis=0)
 
     payload = pl.pallas_call(

time: 143 us -> 143 us (level)
  no operation moved by 1% of the time
where the time goes in v2:
time: 143 us; the launch traced here: 142 us
  starting transfers between devices  50.4 us (35%)
  waiting for transfers between devices  29.7 us (21%)
  blocking collectives  19.8 us (14%)
  Pallas kernels  16 us (11%)
  between operations  14.4 us (10%)
  local copies, waits for them, and re-layouts  11.4 us (8%)
    ppermute x16, starting transfers between devices, shift_ctx(): return lax.ppermute(array, 'ctx', pairs)  50.4 us
    ppermute x16, waiting for transfers between devices, shift_ctx(): return lax.ppermute(array, 'ctx', pairs)  29 us
    all_to_all x1, blocking collectives, body(): lax.all_to_all(merged, 'ctx', 0, 0, axis_index_groups=same, tiled=True)  19.8 us
    unnamed x28, local copies, waits for them, and re-layouts  8.09 us
    pallas_call x1, Pallas kernels, body(): pl.pallas_call(project_kernel, out_shape=(jax.ShapeDtypeStruct((NZ, rows,...  6.74 us
    pallas_call x1, Pallas kernels, body(): pl.pallas_call(fused_kernel, out_shape=(jax.ShapeDtypeStruct((rows, width...  6.4 us
  transfers between devices with their start and end apart: 17, of which 8 were waited for; matrix products, arithmetic and copies ran while one was open for 3% of the time, Pallas kernels for 5%

profile of v2, /device:TPU:392, one launch (start us, length us, event | category | flops | bytes accessed | tf_op | source)
XLA Modules:
  0.0 142.4 jit_solution(7269173493790549867)
XLA Ops:
  7.2 0.0 copy-start
  7.2 0.0 all-gather.3.cloned.1.call-start
  7.2 0.7 all-gather.3.cloned.1.call-update
  7.9 0.8 copy-done.7
  8.8 0.8 copy-done.8
  9.6 0.7 copy-done.11
  10.3 6.7 %collective-permute-start.3 = (bf16[136,512]{1,0:T(8,128)(2,1)S(1)}, bf16[136,512]{1,0:T(8,128)(2,1)S(1)}, u32[]{:S(2)}, u32[]{:S(2)}) collective-permute-start(bf16[136,512]{1,0:T(8,128)(2,1)S(1)} %payload.1.refs_0_), channel_id=1, source_target_pairs={{0,192},{8,200},{16,208},{24,216},{32,224},{40,232},{48,240},{56,2... | collective-permute-start | bytes 417800 | tf_op jit(solution)/shard_map/ppermute | solution.py:25
  17.0 1.9 %collective-permute-start = (bf16[136,512]{1,0:T(8,128)(2,1)S(1)}, bf16[136,512]{1,0:T(8,128)(2,1)S(1)}, u32[]{:S(2)}, u32[]{:S(2)}) collective-permute-start(bf16[136,512]{1,0:T(8,128)(2,1)S(1)} %payload.1.refs_0_), channel_id=1, source_target_pairs={{0,448},{8,456},{16,464},{24,472},{32,480},{40,488},{48,496},{56,5... | collective-permute-start | bytes 417800 | tf_op jit(solution)/shard_map/ppermute | solution.py:25
  19.0 2.7 %collective-permute-start.1 = (bf16[136,512]{1,0:T(8,128)(2,1)S(1)}, bf16[136,512]{1,0:T(8,128)(2,1)S(1)}, u32[]{:S(2)}, u32[]{:S(2)}) collective-permute-start(bf16[136,512]{1,0:T(8,128)(2,1)S(1)} %payload.1.refs_0_), channel_id=1, source_target_pairs={{0,384},{8,392},{16,400},{24,408},{32,416},{40,424},{48,432},{56,4... | collective-permute-start | bytes 417800 | tf_op jit(solution)/shard_map/ppermute | solution.py:25
  21.7 6.0 %collective-permute-start.2 = (bf16[136,512]{1,0:T(8,128)(2,1)S(1)}, bf16[136,512]{1,0:T(8,128)(2,1)S(1)}, u32[]{:S(2)}, u32[]{:S(2)}) collective-permute-start(bf16[136,512]{1,0:T(8,128)(2,1)S(1)} %payload.1.refs_0_), channel_id=1, source_target_pairs={{0,320},{8,328},{16,336},{24,344},{32,352},{40,360},{48,368},{56,3... | collective-permute-start | bytes 417800 | tf_op jit(solution)/shard_map/ppermute | solution.py:25
  27.7 1.9 %collective-permute-start.5 = (bf16[136,512]{1,0:T(8,128)(2,1)S(1)}, bf16[136,512]{1,0:T(8,128)(2,1)S(1)}, u32[]{:S(2)}, u32[]{:S(2)}) collective-permute-start(bf16[136,512]{1,0:T(8,128)(2,1)S(1)} %payload.1.refs_0_), channel_id=1, source_target_pairs={{0,128},{8,136},{16,144},{24,152},{32,160},{40,168},{48,176},{56,1... | collective-permute-start | bytes 417800 | tf_op jit(solution)/shard_map/ppermute | solution.py:25
  29.6 1.2 dynamic_slice.9
  30.9 3.3 %collective-permute-start.6 = (bf16[136,512]{1,0:T(8,128)(2,1)S(1)}, bf16[136,512]{1,0:T(8,128)(2,1)S(1)}, u32[]{:S(2)}, u32[]{:S(2)}) collective-permute-start(bf16[136,512]{1,0:T(8,128)(2,1)S(1)} %payload.1.refs_0_), channel_id=1, source_target_pairs={{0,64},{8,72},{16,80},{24,88},{32,96},{40,104},{48,112},{56,120},{... | collective-permute-start | bytes 417800 | tf_op jit(solution)/shard_map/ppermute | solution.py:25
  34.3 3.5 %collective-permute-start.4 = (bf16[136,512]{1,0:T(8,128)(2,1)S(1)}, bf16[136,512]{1,0:T(8,128)(2,1)S(1)}, u32[]{:S(2)}, u32[]{:S(2)}) collective-permute-start(bf16[136,512]{1,0:T(8,128)(2,1)S(1)} %collective-permute-done.3.refs_5_), channel_id=1, source_target_pairs={{0,64},{8,72},{16,80},{24,88},{32,96},{40,104},{48,112},{56,120},{... | collective-permute-start | bytes 417800 | tf_op jit(solution)/shard_map/ppermute | solution.py:25
  37.7 0.7 iota_compare_fusion.1
  38.5 0.2 dynamic-slice_reduce_fusion
  38.6 0.1 fusion.1
  38.8 0.1 concatenate.3.pos.refs_0_
  38.9 0.7 collective-permute-done.2.refs_3_
  39.6 0.6 collective-permute-done.5.refs_6_
  40.2 0.5 collective-permute-done.6.refs_7_
  40.7 2.2 %collective-permute-done.4.refs_4_ = bf16[136,512]{1,0:T(8,128)(2,1)S(1)} collective-permute-done((bf16[136,512]{1,0:T(8,128)(2,1)S(1)}, bf16[136,512]{1,0:T(8,128)(2,1)S(1)}, u32[]{:S(2)}, u32[]{:S(2)}) %collective-permute-start.4) | collective-permute-done | bytes 139296 | tf_op jit(solution)/shard_map/ppermute | solution.py:25
  42.9 0.6 column.1.own.refs_7_
  43.6 4.7 %collective-permute-start.8 = (bf16[17,64,512]{2,1,0:T(8,128)(2,1)S(1)}, bf16[17,64,512]{2,1,0:T(8,128)(2,1)S(1)}, u32[]{:S(2)}, u32[]{:S(2)}) collective-permute-start(bf16[17,64,512]{2,1,0:T(8,128)(2,1)S(1)} %column.1.own.refs_7_), channel_id=1, source_target_pairs={{0,48},{8,56},{16,0},{24,8},{32,16},{40,24},{48,32},{56,40},{64,11... | collective-permute-start | bytes 3342344 | tf_op jit(solution)/shard_map/ppermute | solution.py:25
  48.3 1.9 %collective-permute-start.9 = (bf16[17,64,512]{2,1,0:T(8,128)(2,1)S(1)}, bf16[17,64,512]{2,1,0:T(8,128)(2,1)S(1)}, u32[]{:S(2)}, u32[]{:S(2)}) collective-permute-start(bf16[17,64,512]{2,1,0:T(8,128)(2,1)S(1)} %column.1.own.refs_7_), channel_id=1, source_target_pairs={{0,16},{8,24},{16,32},{24,40},{32,48},{40,56},{48,0},{56,8},{64,80... | collective-permute-start | bytes 3342344 | tf_op jit(solution)/shard_map/ppermute | solution.py:25
  50.2 1.9 %collective-permute-start.7 = (bf16[17,64,512]{2,1,0:T(8,128)(2,1)S(1)}, bf16[17,64,512]{2,1,0:T(8,128)(2,1)S(1)}, u32[]{:S(2)}, u32[]{:S(2)}) collective-permute-start(bf16[17,64,512]{2,1,0:T(8,128)(2,1)S(1)} %column.1.own.refs_7_), channel_id=1, source_target_pairs={{0,8},{8,0},{16,24},{24,16},{32,40},{40,32},{48,56},{56,48},{64,72... | collective-permute-start | bytes 3342344 | tf_op jit(solution)/shard_map/ppermute | solution.py:25
  52.1 19.6 %collective-permute-done.8.following = bf16[17,64,512]{2,1,0:T(8,128)(2,1)S(1)} collective-permute-done((bf16[17,64,512]{2,1,0:T(8,128)(2,1)S(1)}, bf16[17,64,512]{2,1,0:T(8,128)(2,1)S(1)}, u32[]{:S(2)}, u32[]{:S(2)}) %collective-permute-start.8) | collective-permute-done | bytes 1114144 | tf_op jit(solution)/shard_map/ppermute | solution.py:25
  71.7 0.9 slice.9
  72.6 5.6 %collective-permute-start.11 = (bf16[9,64,512]{2,1,0:T(8,128)(2,1)}, bf16[9,64,512]{2,1,0:T(8,128)(2,1)S(1)}, u32[]{:S(2)}, u32[]{:S(2)}) collective-permute-start(bf16[9,64,512]{2,1,0:T(8,128)(2,1)} %slice.9), channel_id=1, source_target_pairs={{0,48},{8,56},{16,0},{24,8},{32,16},{40,24},{48,32},{56,40},{64,11... | collective-permute-start | bytes 1769480 | tf_op jit(solution)/shard_map/ppermute | solution.py:25
  78.2 0.8 slice.8
  79.1 1.0 copy-done.5
  80.1 1.9 %collective-permute-start.10 = (bf16[8,64,512]{2,1,0:T(8,128)(2,1)}, bf16[8,64,512]{2,1,0:T(8,128)(2,1)S(1)}, u32[]{:S(2)}, u32[]{:S(2)}) collective-permute-start(bf16[8,64,512]{2,1,0:T(8,128)(2,1)} %slice.8), channel_id=1, source_target_pairs={{0,16},{8,24},{16,32},{24,40},{32,48},{40,56},{48,0},{56,8},{64,80... | collective-permute-start | bytes 1572872 | tf_op jit(solution)/shard_map/ppermute | solution.py:25
  82.0 0.0 all-gather.3.cloned.1.call-done
  82.1 1.2 copy-done.4
  83.3 1.2 copy-done.6
  84.6 2.2 %copy-done.12 = bf16[4096,512]{1,0:T(8,128)(2,1)S(1)} copy-done((bf16[4096,512]{1,0:T(8,128)(2,1)S(1)}, bf16[4096,512]{1,0:T(8,128)(2,1)}, u32[]{:S(2)}) %copy-start.12) | copy-done | bytes 4194328
  86.8 6.7 %norm_project.1 = (bf16[8,512,512]{2,1,0:T(8,128)(2,1)S(1)}, f32[512,1024]{1,0:T(8,128)S(1)}, bf16[2,17,64,512]{3,2,1,0:T(8,128)(2,1)S(1)}) custom-call(s32[8]{0:T(128)S(1)} %concatenate.3.pos.refs_0_, f32[8,512]{1,0:T(8,128)S(1)} %reshape.20.gain, bf16[8,512,512]{2,1,0:T(8,128)(2,1)S(1)} %bitcast.10, bf16[17,64,512]{2,1,0:T(8,128)(2,1)S(1)} %column.1.own.refs_7_, ...), custom_call_target="tpu_custom_call" | custom-call | flops 3221225472 | bytes 25165824 | tf_op jit(solution)/shard_map/norm_project/pallas_call | solution.py:228
  93.5 2.0 %collective-permute-done.10.refs_11_ = bf16[8,64,512]{2,1,0:T(8,128)(2,1)S(1)} collective-permute-done((bf16[8,64,512]{2,1,0:T(8,128)(2,1)}, bf16[8,64,512]{2,1,0:T(8,128)(2,1)S(1)}, u32[]{:S(2)}, u32[]{:S(2)}) %collective-permute-start.10) | collective-permute-done | bytes 524320 | tf_op jit(solution)/shard_map/ppermute | solution.py:25
  95.5 1.9 %collective-permute-start.12 = (bf16[2,17,64,512]{3,2,1,0:T(8,128)(2,1)S(1)}, bf16[2,17,64,512]{3,2,1,0:T(8,128)(2,1)S(1)}, u32[]{:S(2)}, u32[]{:S(2)}) collective-permute-start(bf16[2,17,64,512]{3,2,1,0:T(8,128)(2,1)S(1)} %get-tuple-element.14.refs_9_), channel_id=1, source_target_pairs={{0,8},{8,0},{16,24},{24,16},{32,40},{40,32},{48,56},{56,48},{64,72... | collective-permute-start | bytes 6684680 | tf_op jit(solution)/shard_map/ppermute | solution.py:25
  97.4 2.4 %collective-permute-start.14 = (bf16[9,64,512]{2,1,0:T(8,128)(2,1)S(1)}, bf16[9,64,512]{2,1,0:T(8,128)(2,1)S(1)}, u32[]{:S(2)}, u32[]{:S(2)}) collective-permute-start(bf16[9,64,512]{2,1,0:T(8,128)(2,1)S(1)} %collective-permute-done.11.refs_13_), channel_id=1, source_target_pairs={{0,8},{8,0},{16,24},{24,16},{32,40},{40,32},{48,56},{56,48},{64,72... | collective-permute-start | bytes 1769480 | tf_op jit(solution)/shard_map/ppermute | solution.py:25
  99.8 1.9 %collective-permute-start.13 = (bf16[8,64,512]{2,1,0:T(8,128)(2,1)S(1)}, bf16[8,64,512]{2,1,0:T(8,128)(2,1)S(1)}, u32[]{:S(2)}, u32[]{:S(2)}) collective-permute-start(bf16[8,64,512]{2,1,0:T(8,128)(2,1)S(1)} %collective-permute-done.10.refs_11_), channel_id=1, source_target_pairs={{0,8},{8,0},{16,24},{24,16},{32,40},{40,32},{48,56},{56,48},{64,72... | collective-permute-start | bytes 1572872 | tf_op jit(solution)/shard_map/ppermute | solution.py:25
  101.7 1.9 %collective-permute-done.13.refs_12_ = bf16[8,64,512]{2,1,0:T(8,128)(2,1)S(1)} collective-permute-done((bf16[8,64,512]{2,1,0:T(8,128)(2,1)S(1)}, bf16[8,64,512]{2,1,0:T(8,128)(2,1)S(1)}, u32[]{:S(2)}, u32[]{:S(2)}) %collective-permute-start.13) | collective-permute-done | bytes 524320 | tf_op jit(solution)/shard_map/ppermute | solution.py:25
  103.7 6.4 %refresh_attend.1 = (bf16[512,512]{1,0:T(8,128)(2,1)}, bf16[512,512]{1,0:T(8,128)(2,1)}, bf16[256,640]{1,0:T(8,128)(2,1)S(1)}, bf16[256,640]{1,0:T(8,128)(2,1)S(1)}) custom-call(s32[8]{0:T(128)S(1)} %concatenate.3.pos.refs_0_, bf16[512,512]{1,0:T(8,128)(2,1)S(1)} %copy-done.1, bf16[512,512]{1,0:T(8,128)(2,1)S(1)} %copy-done.2, bf16[8,512]{1,0:T(8,128)(2,1)S(1)} %copy-done.9, ...), custom_call_target="tpu_custom_call" | custom-call | flops 3221225472 | bytes 12582912 | tf_op jit(solution)/shard_map/refresh_attend/pallas_call | solution.py:246
  110.1 2.0 %collective-permute-start.15 = (bf16[256,640]{1,0:T(8,128)(2,1)S(1)}, bf16[256,640]{1,0:T(8,128)(2,1)S(1)}, u32[]{:S(2)}, u32[]{:S(2)}) collective-permute-start(bf16[256,640]{1,0:T(8,128)(2,1)S(1)} %get-tuple-element.18), channel_id=1, source_target_pairs={{0,8},{8,0},{16,24},{24,16},{32,40},{40,32},{48,56},{56,48},{64,72... | collective-permute-start | bytes 983048 | tf_op jit(solution)/shard_map/ppermute | solution.py:25
  112.1 1.5 %collective-permute-done.15.two = bf16[256,640]{1,0:T(8,128)(2,1)S(1)} collective-permute-done((bf16[256,640]{1,0:T(8,128)(2,1)S(1)}, bf16[256,640]{1,0:T(8,128)(2,1)S(1)}, u32[]{:S(2)}, u32[]{:S(2)}) %collective-permute-start.15) | collective-permute-done | bytes 327712 | tf_op jit(solution)/shard_map/ppermute | solution.py:25
  113.6 1.0 merge.1
  114.6 19.8 %all_to_all.11 = bf16[32,8,640]{2,1,0:T(8,128)(2,1)S(1)} all-to-all(bf16[32,8,640]{2,1,0:T(8,128)(2,1)S(1)} %bitcast.9), channel_id=1, replica_groups={{0,64,128,192,256,320,384,448,16,80,144,208,272,336,400,464,32,96,160,2..., dimensions={0} | all-to-all | bytes 655360 | tf_op jit(solution)/shard_map/all_to_all | solution.py:291
  134.4 1.2 combine.1
  (31 shorter events, 0.1 us)
Async XLA Ops:
  7.2 31.3 %copy-start = (s32[64,4]{0,1:T(4,128)S(1)}, s32[64,4]{0,1:T(4,128)}, u32[]{:S(2)}) copy-start(s32[64,4]{0,1:T(4,128)} %param.20) | copy-start | bytes 3076
  7.2 74.9 %all-gather.3.cloned.1.call-start = ((), (), s32[]{:S(2)}) async-start(), calls=%async_computation.1 | async-start | bytes 4718592 | tf_op jit(solution)/shard_map/all_gather | solution.py:204
  7.9 0.8 copy-start.7
  8.8 0.8 copy-start.8
  9.6 0.7 copy-start.11
  10.3 20.6 %collective-permute-start.3 = (bf16[136,512]{1,0:T(8,128)(2,1)S(1)}, bf16[136,512]{1,0:T(8,128)(2,1)S(1)}, u32[]{:S(2)}, u32[]{:S(2)}) collective-permute-start(bf16[136,512]{1,0:T(8,128)(2,1)S(1)} %payload.1.refs_0_), channel_id=1, source_target_pairs={{0,192},{8,200},{16,208},{24,216},{32,224},{40,232},{48,240},{56,2... | collective-permute-start | bytes 417800 | tf_op jit(solution)/shard_map/ppermute | solution.py:25
  17.0 17.2 %collective-permute-start = (bf16[136,512]{1,0:T(8,128)(2,1)S(1)}, bf16[136,512]{1,0:T(8,128)(2,1)S(1)}, u32[]{:S(2)}, u32[]{:S(2)}) collective-permute-start(bf16[136,512]{1,0:T(8,128)(2,1)S(1)} %payload.1.refs_0_), channel_id=1, source_target_pairs={{0,448},{8,456},{16,464},{24,472},{32,480},{40,488},{48,496},{56,5... | collective-permute-start | bytes 417800 | tf_op jit(solution)/shard_map/ppermute | solution.py:25
  19.0 19.9 %collective-permute-start.1 = (bf16[136,512]{1,0:T(8,128)(2,1)S(1)}, bf16[136,512]{1,0:T(8,128)(2,1)S(1)}, u32[]{:S(2)}, u32[]{:S(2)}) collective-permute-start(bf16[136,512]{1,0:T(8,128)(2,1)S(1)} %payload.1.refs_0_), channel_id=1, source_target_pairs={{0,384},{8,392},{16,400},{24,408},{32,416},{40,424},{48,432},{56,4... | collective-permute-start | bytes 417800 | tf_op jit(solution)/shard_map/ppermute | solution.py:25
  21.7 18.0 %collective-permute-start.2 = (bf16[136,512]{1,0:T(8,128)(2,1)S(1)}, bf16[136,512]{1,0:T(8,128)(2,1)S(1)}, u32[]{:S(2)}, u32[]{:S(2)}) collective-permute-start(bf16[136,512]{1,0:T(8,128)(2,1)S(1)} %payload.1.refs_0_), channel_id=1, source_target_pairs={{0,320},{8,328},{16,336},{24,344},{32,352},{40,360},{48,368},{56,3... | collective-permute-start | bytes 417800 | tf_op jit(solution)/shard_map/ppermute | solution.py:25
  27.7 12.5 %collective-permute-start.5 = (bf16[136,512]{1,0:T(8,128)(2,1)S(1)}, bf16[136,512]{1,0:T(8,128)(2,1)S(1)}, u32[]{:S(2)}, u32[]{:S(2)}) collective-permute-start(bf16[136,512]{1,0:T(8,128)(2,1)S(1)} %payload.1.refs_0_), channel_id=1, source_target_pairs={{0,128},{8,136},{16,144},{24,152},{32,160},{40,168},{48,176},{56,1... | collective-permute-start | bytes 417800 | tf_op jit(solution)/shard_map/ppermute | solution.py:25
  30.9 9.8 %collective-permute-start.6 = (bf16[136,512]{1,0:T(8,128)(2,1)S(1)}, bf16[136,512]{1,0:T(8,128)(2,1)S(1)}, u32[]{:S(2)}, u32[]{:S(2)}) collective-permute-start(bf16[136,512]{1,0:T(8,128)(2,1)S(1)} %payload.1.refs_0_), channel_id=1, source_target_pairs={{0,64},{8,72},{16,80},{24,88},{32,96},{40,104},{48,112},{56,120},{... | collective-permute-start | bytes 417800 | tf_op jit(solution)/shard_map/ppermute | solution.py:25
  34.3 8.7 %collective-permute-start.4 = (bf16[136,512]{1,0:T(8,128)(2,1)S(1)}, bf16[136,512]{1,0:T(8,128)(2,1)S(1)}, u32[]{:S(2)}, u32[]{:S(2)}) collective-permute-start(bf16[136,512]{1,0:T(8,128)(2,1)S(1)} %collective-permute-done.3.refs_5_), channel_id=1, source_target_pairs={{0,64},{8,72},{16,80},{24,88},{32,96},{40,104},{48,112},{56,120},{... | collective-permute-start | bytes 417800 | tf_op jit(solution)/shard_map/ppermute | solution.py:25
  38.9 43.1 %copy-start.13 = (bf16[4096]{0:T(1024)(128)(2,1)S(1)}, bf16[4096]{0:T(1024)(128)(2,1)}, u32[]{:S(2)}) copy-start(bf16[4096]{0:T(1024)(128)(2,1)} %param.12) | copy-start | bytes 24580
  43.6 28.1 %collective-permute-start.8 = (bf16[17,64,512]{2,1,0:T(8,128)(2,1)S(1)}, bf16[17,64,512]{2,1,0:T(8,128)(2,1)S(1)}, u32[]{:S(2)}, u32[]{:S(2)}) collective-permute-start(bf16[17,64,512]{2,1,0:T(8,128)(2,1)S(1)} %column.1.own.refs_7_), channel_id=1, source_target_pairs={{0,48},{8,56},{16,0},{24,8},{32,16},{40,24},{48,32},{56,40},{64,11... | collective-permute-start | bytes 3342344 | tf_op jit(solution)/shard_map/ppermute | solution.py:25
  48.3 29.9 %collective-permute-start.9 = (bf16[17,64,512]{2,1,0:T(8,128)(2,1)S(1)}, bf16[17,64,512]{2,1,0:T(8,128)(2,1)S(1)}, u32[]{:S(2)}, u32[]{:S(2)}) collective-permute-start(bf16[17,64,512]{2,1,0:T(8,128)(2,1)S(1)} %column.1.own.refs_7_), channel_id=1, source_target_pairs={{0,16},{8,24},{16,32},{24,40},{32,48},{40,56},{48,0},{56,8},{64,80... | collective-permute-start | bytes 3342344 | tf_op jit(solution)/shard_map/ppermute | solution.py:25
  50.2 31.8 %collective-permute-start.7 = (bf16[17,64,512]{2,1,0:T(8,128)(2,1)S(1)}, bf16[17,64,512]{2,1,0:T(8,128)(2,1)S(1)}, u32[]{:S(2)}, u32[]{:S(2)}) collective-permute-start(bf16[17,64,512]{2,1,0:T(8,128)(2,1)S(1)} %column.1.own.refs_7_), channel_id=1, source_target_pairs={{0,8},{8,0},{16,24},{24,16},{32,40},{40,32},{48,56},{56,48},{64,72... | collective-permute-start | bytes 3342344 | tf_op jit(solution)/shard_map/ppermute | solution.py:25
  71.7 6.5 %copy-start.3 = (bf16[17,64,512]{2,1,0:T(8,128)(2,1)}, bf16[17,64,512]{2,1,0:T(8,128)(2,1)S(1)}, u32[]{:S(2)}) copy-start(bf16[17,64,512]{2,1,0:T(8,128)(2,1)S(1)} %collective-permute-done.8.following) | copy-start | bytes 3342340
  72.6 22.9 %collective-permute-start.11 = (bf16[9,64,512]{2,1,0:T(8,128)(2,1)}, bf16[9,64,512]{2,1,0:T(8,128)(2,1)S(1)}, u32[]{:S(2)}, u32[]{:S(2)}) collective-permute-start(bf16[9,64,512]{2,1,0:T(8,128)(2,1)} %slice.9), channel_id=1, source_target_pairs={{0,48},{8,56},{16,0},{24,8},{32,16},{40,24},{48,32},{56,40},{64,11... | collective-permute-start | bytes 1769480 | tf_op jit(solution)/shard_map/ppermute | solution.py:25
  79.1 1.0 copy-start.5
  80.1 15.4 %collective-permute-start.10 = (bf16[8,64,512]{2,1,0:T(8,128)(2,1)}, bf16[8,64,512]{2,1,0:T(8,128)(2,1)S(1)}, u32[]{:S(2)}, u32[]{:S(2)}) collective-permute-start(bf16[8,64,512]{2,1,0:T(8,128)(2,1)} %slice.8), channel_id=1, source_target_pairs={{0,16},{8,24},{16,32},{24,40},{32,48},{40,56},{48,0},{56,8},{64,80... | collective-permute-start | bytes 1572872 | tf_op jit(solution)/shard_map/ppermute | solution.py:25
  82.1 1.2 copy-start.4
  83.3 1.2 copy-start.6
  84.6 2.2 %copy-start.12 = (bf16[4096,512]{1,0:T(8,128)(2,1)S(1)}, bf16[4096,512]{1,0:T(8,128)(2,1)}, u32[]{:S(2)}) copy-start(bf16[4096,512]{1,0:T(8,128)(2,1)} %all-gather.3.cloned.1.call-done) | copy-start | bytes 12582916
  86.7 16.9 %copy-start.1 = (bf16[512,512]{1,0:T(8,128)(2,1)S(1)}, bf16[512,512]{1,0:T(8,128)(2,1)}, u32[]{:S(2)}) copy-start(bf16[512,512]{1,0:T(8,128)(2,1)} %refs_1_.1) | copy-start | bytes 1572868
  86.8 16.9 %copy-start.2 = (bf16[512,512]{1,0:T(8,128)(2,1)S(1)}, bf16[512,512]{1,0:T(8,128)(2,1)}, u32[]{:S(2)}) copy-start(bf16[512,512]{1,0:T(8,128)(2,1)} %refs_2_.1) | copy-start | bytes 1572868
  86.8 16.9 %copy-start.9 = (bf16[8,512]{1,0:T(8,128)(2,1)S(1)}, bf16[8,512]{1,0:T(8,128)(2,1)}, u32[]{:S(2)}) copy-start(bf16[8,512]{1,0:T(8,128)(2,1)} %refs_3_.1) | copy-start | bytes 24580
  86.8 16.9 %copy-start.10 = (bf16[8,512]{1,0:T(8,128)(2,1)S(1)}, bf16[8,512]{1,0:T(8,128)(2,1)}, u32[]{:S(2)}) copy-start(bf16[8,512]{1,0:T(8,128)(2,1)} %refs_4_.1) | copy-start | bytes 24580
  95.5 8.1 %collective-permute-start.12 = (bf16[2,17,64,512]{3,2,1,0:T(8,128)(2,1)S(1)}, bf16[2,17,64,512]{3,2,1,0:T(8,128)(2,1)S(1)}, u32[]{:S(2)}, u32[]{:S(2)}) collective-permute-start(bf16[2,17,64,512]{3,2,1,0:T(8,128)(2,1)S(1)} %get-tuple-element.14.refs_9_), channel_id=1, source_target_pairs={{0,8},{8,0},{16,24},{24,16},{32,40},{40,32},{48,56},{56,48},{64,72... | collective-permute-start | bytes 6684680 | tf_op jit(solution)/shard_map/ppermute | solution.py:25
  97.4 6.2 %collective-permute-start.14 = (bf16[9,64,512]{2,1,0:T(8,128)(2,1)S(1)}, bf16[9,64,512]{2,1,0:T(8,128)(2,1)S(1)}, u32[]{:S(2)}, u32[]{:S(2)}) collective-permute-start(bf16[9,64,512]{2,1,0:T(8,128)(2,1)S(1)} %collective-permute-done.11.refs_13_), channel_id=1, source_target_pairs={{0,8},{8,0},{16,24},{24,16},{32,40},{40,32},{48,56},{56,48},{64,72... | collective-permute-start | bytes 1769480 | tf_op jit(solution)/shard_map/ppermute | solution.py:25
  99.8 3.8 %collective-permute-start.13 = (bf16[8,64,512]{2,1,0:T(8,128)(2,1)S(1)}, bf16[8,64,512]{2,1,0:T(8,128)(2,1)S(1)}, u32[]{:S(2)}, u32[]{:S(2)}) collective-permute-start(bf16[8,64,512]{2,1,0:T(8,128)(2,1)S(1)} %collective-permute-done.10.refs_11_), channel_id=1, source_target_pairs={{0,8},{8,0},{16,24},{24,16},{32,40},{40,32},{48,56},{56,48},{64,72... | collective-permute-start | bytes 1572872 | tf_op jit(solution)/shard_map/ppermute | solution.py:25
  110.1 3.5 %collective-permute-start.15 = (bf16[256,640]{1,0:T(8,128)(2,1)S(1)}, bf16[256,640]{1,0:T(8,128)(2,1)S(1)}, u32[]{:S(2)}, u32[]{:S(2)}) collective-permute-start(bf16[256,640]{1,0:T(8,128)(2,1)S(1)} %get-tuple-element.18), channel_id=1, source_target_pairs={{0,8},{8,0},{16,24},{24,16},{32,40},{40,32},{48,56},{56,48},{64,72... | collective-permute-start | bytes 983048 | tf_op jit(solution)/shard_map/ppermute | solution.py:25
Sparse Core Ops, SparseCore 0:
  10.1 55.7 all-gather.2

commit v3 on v2

--- a/solution.py
+++ b/solution.py
@@ -40,7 +40,8 @@
 
 
 def column_kernel(pos, *refs):
-    pieces, out, held = refs[:NY], refs[NY], refs[NY + 1]
+    pieces, gain, out, gain_out, held = refs[:NY], *refs[NY:]
+    gain_out[...] = gain[...]
     y = pos[0]
     for a, piece in enumerate(pieces):
         row = lax.rem(y + a, NY)
@@ -48,6 +49,15 @@
         out[NY + row] = piece[WROWS : 2 * WROWS, :]
         held[pl.ds(pl.multiple_of(row * 8, 8), 8), :] = piece[2 * WROWS :, :].astype(F32)
     out[2 * NY] = held[...].astype(BF16)
+
+
+def part_kernel(first, piece, out):
+    out[...] = piece[first : first + out.shape[0]]
+
+
+def join_kernel(one, two, out):
+    out[: one.shape[0]] = one[...]
+    out[one.shape[0] :] = two[...]
 
 
 def payload_kernel(keys, values, queries, out):
@@ -93,22 +103,22 @@
 
 def fused_kernel(*refs):
     pos, cache_k, cache_v, resp_k, resp_v, normed, acc_in = refs[:7]
-    own, own_sw, pair, pair_sw, far_k, far_k_sw, far_v, far_v_sw = refs[7:15]
-    new_k, new_v, packed_mine, packed_other, queries, keys, values, acc = refs[15:]
+    own, own_sw, pair, pair_sw, far, far_sw = refs[7:13]
+    new_k, new_v, packed_mine, packed_other, queries, keys, values, acc = refs[13:]
     rows, depth = normed.shape[1:]
     width = own.shape[2]
     x = pos[1]
     place = place_from(pos)
 
-    for e, (mine, two, far) in enumerate(((own, pair, far_v), (own_sw, pair_sw, far_v_sw))):
-        for b, block in enumerate((mine[2 * NY], two[0, 2 * NY], far[NY], two[1, 2 * NY])):
+    for e, (mine, two, third) in enumerate(((own, pair, far), (own_sw, pair_sw, far_sw))):
+        for b, block in enumerate((mine[2 * NY], two[0, 2 * NY], third[2 * NY], two[1, 2 * NY])):
             queries[e * NX + lax.rem(x + b, NX)] = block
     acc[...] = acc_in[...]
     for left, of_k, of_v in (
         (place(1, 1), pair_sw[0, :NY], pair_sw[0, NY : 2 * NY]),
         (place(3, 1), pair_sw[1, :NY], pair_sw[1, NY : 2 * NY]),
-        (place(2, 0), far_k[...], far_v[:NY]),
-        (place(2, 1), far_k_sw[...], far_v_sw[:NY]),
+        (place(2, 0), far[:NY], far[NY : 2 * NY]),
+        (place(2, 1), far_sw[:NY], far_sw[NY : 2 * NY]),
     ):
         acc[:, :width] += jnp.dot(normed[left], of_k.reshape(depth, width), preferred_element_type=F32)
         acc[:, width:] += jnp.dot(normed[left], of_v.reshape(depth, width), preferred_element_type=F32)
@@ -213,17 +223,33 @@
     )(key_weight, value_weight, resp_queries)
     near = {a: shift_ctx(payload, dy=-a) for a in (3, 5, 2, 6, 1, 7)}
     near[4] = shift_ctx(near[5], dy=1)
-    column = pl.pallas_call(
+    column, gain = pl.pallas_call(
         column_kernel,
-        out_shape=jax.ShapeDtypeStruct((2 * NY + 1, WROWS, width), BF16),
-        in_specs=[smem] + [vmem] * NY,
-        out_specs=vmem,
+        out_shape=(
+            jax.ShapeDtypeStruct((2 * NY + 1, WROWS, width), BF16),
+            jax.ShapeDtypeStruct((NZ, slice_width), F32),
+        ),
+        in_specs=[smem] + [vmem] * (NY + 1),
+        out_specs=(vmem, vmem),
         scratch_shapes=[pltpu.VMEM((NY * resp_queries.shape[0], width), F32)],
         compiler_params=pltpu.CompilerParams(vmem_limit_bytes=16 << 20),
         name="column",
-    )(pos, payload, *[near[a] for a in range(1, NY)])
+    )(pos, payload, *[near[a] for a in range(1, NY)], norm_gain.astype(F32).reshape(NZ, slice_width))
+
+    small = pltpu.CompilerParams(vmem_limit_bytes=8 << 20)
+
+    def part(piece, first, count):
+        return pl.pallas_call(
+            lambda *refs: part_kernel(first, *refs),
+            out_shape=jax.ShapeDtypeStruct((count,) + piece.shape[1:], BF16),
+            in_specs=[vmem],
+            out_specs=vmem,
+            compiler_params=small,
+            name="part",
+        )(piece)
+
     following, last = shift_ctx(column, dx=-1), shift_ctx(column, dx=1)
-    far_k, far_v = shift_ctx(last[:NY], dx=1), shift_ctx(following[NY:], dx=-1)
+    far_k, far_v = shift_ctx(part(last, 0, NY), dx=1), shift_ctx(part(following, NY, NY + 1), dx=-1)
     own_sw = shift_ctx(column, dcore=1)
     normed, partial, pair = pl.pallas_call(
         project_kernel,
@@ -237,9 +263,17 @@
         compiler_params=big,
         cost_estimate=pl.CostEstimate(flops=3 << 30, bytes_accessed=24 << 20, transcendentals=512),
         name="norm_project",
-    )(pos, norm_gain.astype(F32).reshape(NZ, slice_width), x_all, column, own_sw, following, last)
+    )(pos, gain, x_all, column, own_sw, following, last)
     pair_sw = shift_ctx(lax.optimization_barrier((pair, far_k, far_v))[0], dcore=1)
-    far_k_sw, far_v_sw = shift_ctx(far_k, dcore=1), shift_ctx(far_v, dcore=1)
+    far = pl.pallas_call(
+        join_kernel,
+        out_shape=jax.ShapeDtypeStruct(column.shape, BF16),
+        in_specs=[vmem] * 2,
+        out_specs=vmem,
+        compiler_params=small,
+        name="join",
+    )(far_k, far_v)
+    far_sw = shift_ctx(far, dcore=1)
 
     total = 2 * NY * NX * resp_queries.shape[0]
     result = jax.ShapeDtypeStruct((total // 2, width + 128), BF16)
@@ -251,7 +285,7 @@
             result,
             result,
         ),
-        in_specs=[smem] + [vmem] * 14,
+        in_specs=[smem] + [vmem] * 12,
         out_specs=(vmem, vmem, vmem, vmem),
         scratch_shapes=[
             pltpu.VMEM((2 * NX, WROWS, width), BF16),
@@ -274,10 +308,8 @@
         own_sw,
         pair,
         pair_sw,
-        far_k,
-        far_k_sw,
-        far_v,
-        far_v_sw,
+        far,
+        far_sw,
     )
     merged = pl.pallas_call(
         merge_kernel,

time: 143 us -> 142 us (level)
  local copies, waits for them, and re-layouts: 11.4 us -> 8.06 us
  Pallas kernels: 16 us -> 19 us
  starting transfers between devices: 50.4 us -> 48.9 us
    pallas_call x1 -> x4, Pallas kernels: 0.64 us -> 3.66 us  [the longest x2 1.73 us: part(): pl.pallas_call(lambda *refs: part_kernel(first, *refs), out_shape=jax.Sha...]
    unnamed x28 -> x22, local copies, waits for them, and re-layouts: 8.09 us -> 5.83 us
    slice x2 -> x0, local copies, waits for them, and re-layouts: 1.73 us -> none  [the longest x1 0.9 us: body(): following[NY:]]
    ppermute x16 -> x15, starting transfers between devices: 50.4 us -> 48.9 us  [shift_ctx(): return lax.ppermute(array, 'ctx', pairs)]
    ppermute x16 -> x15, waiting for transfers between devices: 29 us -> 29.9 us  [shift_ctx(): return lax.ppermute(array, 'ctx', pairs)]
  transfers between devices with their start and end apart: 17 -> 16, of which waited for: 8 -> 7; matrix products, arithmetic and copies ran while one was open for 3% -> 2% of each run, Pallas kernels for 5% -> 7%
where the time goes in v3:
time: 142 us; the launch traced here: 141 us
  starting transfers between devices  48.9 us (34%)
  waiting for transfers between devices  30.6 us (22%)
  blocking collectives  19.5 us (14%)
  Pallas kernels  19 us (13%)
  between operations  14.3 us (10%)
  local copies, waits for them, and re-layouts  8.06 us (6%)
    ppermute x15, starting transfers between devices, shift_ctx(): return lax.ppermute(array, 'ctx', pairs)  48.9 us
    ppermute x15, waiting for transfers between devices, shift_ctx(): return lax.ppermute(array, 'ctx', pairs)  29.9 us
    all_to_all x1, blocking collectives, body(): lax.all_to_all(merged, 'ctx', 0, 0, axis_index_groups=same, tiled=True)  19.5 us
    pallas_call x1, Pallas kernels, body(): pl.pallas_call(project_kernel, out_shape=(jax.ShapeDtypeStruct((NZ, rows,...  6.74 us
    pallas_call x1, Pallas kernels, body(): pl.pallas_call(fused_kernel, out_shape=(jax.ShapeDtypeStruct((rows, width...  6.4 us
    unnamed x22, local copies, waits for them, and re-layouts  5.83 us
  transfers between devices with their start and end apart: 16, of which 7 were waited for; matrix products, arithmetic and copies ran while one was open for 2% of the time, Pallas kernels for 7%

profile of v3, /device:TPU:392, one launch (start us, length us, event | category | flops | bytes accessed | tf_op | source)
XLA Modules:
  0.0 141.2 jit_solution(4084057442737300745)
XLA Ops:
  7.2 0.0 copy-start
  7.2 0.0 all-gather.3.cloned.1.call-start
  7.2 0.7 all-gather.3.cloned.1.call-update
  7.9 0.8 copy-done.5
  8.8 0.8 copy-done.6
  9.6 0.7 copy-done.9
  10.3 6.7 %collective-permute-start.3 = (bf16[136,512]{1,0:T(8,128)(2,1)S(1)}, bf16[136,512]{1,0:T(8,128)(2,1)S(1)}, u32[]{:S(2)}, u32[]{:S(2)}) collective-permute-start(bf16[136,512]{1,0:T(8,128)(2,1)S(1)} %payload.1.refs_0_), channel_id=1, source_target_pairs={{0,192},{8,200},{16,208},{24,216},{32,224},{40,232},{48,240},{56,2... | collective-permute-start | bytes 417800 | tf_op jit(solution)/shard_map/ppermute | solution.py:25
  17.0 1.9 %collective-permute-start = (bf16[136,512]{1,0:T(8,128)(2,1)S(1)}, bf16[136,512]{1,0:T(8,128)(2,1)S(1)}, u32[]{:S(2)}, u32[]{:S(2)}) collective-permute-start(bf16[136,512]{1,0:T(8,128)(2,1)S(1)} %payload.1.refs_0_), channel_id=1, source_target_pairs={{0,448},{8,456},{16,464},{24,472},{32,480},{40,488},{48,496},{56,5... | collective-permute-start | bytes 417800 | tf_op jit(solution)/shard_map/ppermute | solution.py:25
  19.0 2.7 %collective-permute-start.1 = (bf16[136,512]{1,0:T(8,128)(2,1)S(1)}, bf16[136,512]{1,0:T(8,128)(2,1)S(1)}, u32[]{:S(2)}, u32[]{:S(2)}) collective-permute-start(bf16[136,512]{1,0:T(8,128)(2,1)S(1)} %payload.1.refs_0_), channel_id=1, source_target_pairs={{0,384},{8,392},{16,400},{24,408},{32,416},{40,424},{48,432},{56,4... | collective-permute-start | bytes 417800 | tf_op jit(solution)/shard_map/ppermute | solution.py:25
  21.7 6.0 %collective-permute-start.2 = (bf16[136,512]{1,0:T(8,128)(2,1)S(1)}, bf16[136,512]{1,0:T(8,128)(2,1)S(1)}, u32[]{:S(2)}, u32[]{:S(2)}) collective-permute-start(bf16[136,512]{1,0:T(8,128)(2,1)S(1)} %payload.1.refs_0_), channel_id=1, source_target_pairs={{0,320},{8,328},{16,336},{24,344},{32,352},{40,360},{48,368},{56,3... | collective-permute-start | bytes 417800 | tf_op jit(solution)/shard_map/ppermute | solution.py:25
  27.7 1.9 %collective-permute-start.5 = (bf16[136,512]{1,0:T(8,128)(2,1)S(1)}, bf16[136,512]{1,0:T(8,128)(2,1)S(1)}, u32[]{:S(2)}, u32[]{:S(2)}) collective-permute-start(bf16[136,512]{1,0:T(8,128)(2,1)S(1)} %payload.1.refs_0_), channel_id=1, source_target_pairs={{0,128},{8,136},{16,144},{24,152},{32,160},{40,168},{48,176},{56,1... | collective-permute-start | bytes 417800 | tf_op jit(solution)/shard_map/ppermute | solution.py:25
  29.6 1.2 dynamic_slice.9
  30.9 3.3 %collective-permute-start.6 = (bf16[136,512]{1,0:T(8,128)(2,1)S(1)}, bf16[136,512]{1,0:T(8,128)(2,1)S(1)}, u32[]{:S(2)}, u32[]{:S(2)}) collective-permute-start(bf16[136,512]{1,0:T(8,128)(2,1)S(1)} %payload.1.refs_0_), channel_id=1, source_target_pairs={{0,64},{8,72},{16,80},{24,88},{32,96},{40,104},{48,112},{56,120},{... | collective-permute-start | bytes 417800 | tf_op jit(solution)/shard_map/ppermute | solution.py:25
  34.3 3.5 %collective-permute-start.4 = (bf16[136,512]{1,0:T(8,128)(2,1)S(1)}, bf16[136,512]{1,0:T(8,128)(2,1)S(1)}, u32[]{:S(2)}, u32[]{:S(2)}) collective-permute-start(bf16[136,512]{1,0:T(8,128)(2,1)S(1)} %collective-permute-done.3.refs_5_), channel_id=1, source_target_pairs={{0,64},{8,72},{16,80},{24,88},{32,96},{40,104},{48,112},{56,120},{... | collective-permute-start | bytes 417800 | tf_op jit(solution)/shard_map/ppermute | solution.py:25
  37.7 0.7 iota_compare_fusion.1
  38.5 0.2 dynamic-slice_reduce_fusion
  38.6 0.1 fusion.1
  38.8 0.7 reshape.20.refs_8_
  39.5 0.1 concatenate.3.pos.refs_0_
  39.6 0.0 collective-permute-done.2.refs_3_
  39.6 0.6 collective-permute-done.5.refs_6_
  40.2 0.5 collective-permute-done.6.refs_7_
  40.7 2.2 %collective-permute-done.4.refs_4_ = bf16[136,512]{1,0:T(8,128)(2,1)S(1)} collective-permute-done((bf16[136,512]{1,0:T(8,128)(2,1)S(1)}, bf16[136,512]{1,0:T(8,128)(2,1)S(1)}, u32[]{:S(2)}, u32[]{:S(2)}) %collective-permute-start.4) | collective-permute-done | bytes 139296 | tf_op jit(solution)/shard_map/ppermute | solution.py:25
  42.9 0.6 column.1
  43.6 4.7 %collective-permute-start.8 = (bf16[17,64,512]{2,1,0:T(8,128)(2,1)S(1)}, bf16[17,64,512]{2,1,0:T(8,128)(2,1)S(1)}, u32[]{:S(2)}, u32[]{:S(2)}) collective-permute-start(bf16[17,64,512]{2,1,0:T(8,128)(2,1)S(1)} %get-tuple-element.14.own.refs_7_), channel_id=1, source_target_pairs={{0,48},{8,56},{16,0},{24,8},{32,16},{40,24},{48,32},{56,40},{64,11... | collective-permute-start | bytes 3342344 | tf_op jit(solution)/shard_map/ppermute | solution.py:25
  48.3 1.9 %collective-permute-start.9 = (bf16[17,64,512]{2,1,0:T(8,128)(2,1)S(1)}, bf16[17,64,512]{2,1,0:T(8,128)(2,1)S(1)}, u32[]{:S(2)}, u32[]{:S(2)}) collective-permute-start(bf16[17,64,512]{2,1,0:T(8,128)(2,1)S(1)} %get-tuple-element.14.own.refs_7_), channel_id=1, source_target_pairs={{0,16},{8,24},{16,32},{24,40},{32,48},{40,56},{48,0},{56,8},{64,80... | collective-permute-start | bytes 3342344 | tf_op jit(solution)/shard_map/ppermute | solution.py:25
  50.2 1.9 %collective-permute-start.7 = (bf16[17,64,512]{2,1,0:T(8,128)(2,1)S(1)}, bf16[17,64,512]{2,1,0:T(8,128)(2,1)S(1)}, u32[]{:S(2)}, u32[]{:S(2)}) collective-permute-start(bf16[17,64,512]{2,1,0:T(8,128)(2,1)S(1)} %get-tuple-element.14.own.refs_7_), channel_id=1, source_target_pairs={{0,8},{8,0},{16,24},{24,16},{32,40},{40,32},{48,56},{56,48},{64,72... | collective-permute-start | bytes 3342344 | tf_op jit(solution)/shard_map/ppermute | solution.py:25
  52.1 19.6 %collective-permute-done.8.following.refs_0_ = bf16[17,64,512]{2,1,0:T(8,128)(2,1)S(1)} collective-permute-done((bf16[17,64,512]{2,1,0:T(8,128)(2,1)S(1)}, bf16[17,64,512]{2,1,0:T(8,128)(2,1)S(1)}, u32[]{:S(2)}, u32[]{:S(2)}) %collective-permute-start.8) | collective-permute-done | bytes 1114144 | tf_op jit(solution)/shard_map/ppermute | solution.py:25
  71.7 0.9 part.3
  72.6 5.6 %collective-permute-start.11 = (bf16[9,64,512]{2,1,0:T(8,128)(2,1)}, bf16[9,64,512]{2,1,0:T(8,128)(2,1)}, u32[]{:S(2)}, u32[]{:S(2)}) collective-permute-start(bf16[9,64,512]{2,1,0:T(8,128)(2,1)} %part.3), channel_id=1, source_target_pairs={{0,48},{8,56},{16,0},{24,8},{32,16},{40,24},{48,32},{56,40},{64,11... | collective-permute-start | bytes 1769480 | tf_op jit(solution)/shard_map/ppermute | solution.py:25
  78.2 0.8 part.2
  79.0 1.9 %collective-permute-start.10 = (bf16[8,64,512]{2,1,0:T(8,128)(2,1)}, bf16[8,64,512]{2,1,0:T(8,128)(2,1)}, u32[]{:S(2)}, u32[]{:S(2)}) collective-permute-start(bf16[8,64,512]{2,1,0:T(8,128)(2,1)} %part.2), channel_id=1, source_target_pairs={{0,16},{8,24},{16,32},{24,40},{32,48},{40,56},{48,0},{56,8},{64,80... | collective-permute-start | bytes 1572872 | tf_op jit(solution)/shard_map/ppermute | solution.py:25
  81.0 0.0 all-gather.3.cloned.1.call-done
  81.0 1.2 copy-done.2
  82.3 2.2 %copy-done.10 = bf16[4096,512]{1,0:T(8,128)(2,1)S(1)} copy-done((bf16[4096,512]{1,0:T(8,128)(2,1)S(1)}, bf16[4096,512]{1,0:T(8,128)(2,1)}, u32[]{:S(2)}) %copy-start.10) | copy-done | bytes 4194328
  84.4 6.7 %norm_project.1 = (bf16[8,512,512]{2,1,0:T(8,128)(2,1)S(1)}, f32[512,1024]{1,0:T(8,128)S(1)}, bf16[2,17,64,512]{3,2,1,0:T(8,128)(2,1)S(1)}) custom-call(s32[8]{0:T(128)S(1)} %concatenate.3.pos.refs_0_, f32[8,512]{1,0:T(8,128)S(1)} %get-tuple-element.13.gain, bf16[8,512,512]{2,1,0:T(8,128)(2,1)S(1)} %bitcast.10, ...), custom_call_target="tpu_custom_call" | custom-call | flops 3221225472 | bytes 25165824 | tf_op jit(solution)/shard_map/norm_project/pallas_call | solution.py:254
  91.2 3.4 %collective-permute-done.10.one = bf16[8,64,512]{2,1,0:T(8,128)(2,1)} collective-permute-done((bf16[8,64,512]{2,1,0:T(8,128)(2,1)}, bf16[8,64,512]{2,1,0:T(8,128)(2,1)}, u32[]{:S(2)}, u32[]{:S(2)}) %collective-permute-start.10) | collective-permute-done | bytes 524320 | tf_op jit(solution)/shard_map/ppermute | solution.py:25
  94.6 0.0 copy-start.8
  94.6 2.1 %collective-permute-start.12 = (bf16[2,17,64,512]{3,2,1,0:T(8,128)(2,1)S(1)}, bf16[2,17,64,512]{3,2,1,0:T(8,128)(2,1)S(1)}, u32[]{:S(2)}, u32[]{:S(2)}) collective-permute-start(bf16[2,17,64,512]{3,2,1,0:T(8,128)(2,1)S(1)} %get-tuple-element.18.refs_9_), channel_id=1, source_target_pairs={{0,8},{8,0},{16,24},{24,16},{32,40},{40,32},{48,56},{56,48},{64,72... | collective-permute-start | bytes 6684680 | tf_op jit(solution)/shard_map/ppermute | solution.py:25
  96.6 1.3 join.1.refs_11_
  98.0 2.4 %collective-permute-start.13 = (bf16[17,64,512]{2,1,0:T(8,128)(2,1)S(1)}, bf16[17,64,512]{2,1,0:T(8,128)(2,1)S(1)}, u32[]{:S(2)}, u32[]{:S(2)}) collective-permute-start(bf16[17,64,512]{2,1,0:T(8,128)(2,1)S(1)} %join.1.refs_11_), channel_id=1, source_target_pairs={{0,8},{8,0},{16,24},{24,16},{32,40},{40,32},{48,56},{56,48},{64,72... | collective-permute-start | bytes 3342344 | tf_op jit(solution)/shard_map/ppermute | solution.py:25
  100.4 2.4 %collective-permute-done.13.refs_12_ = bf16[17,64,512]{2,1,0:T(8,128)(2,1)S(1)} collective-permute-done((bf16[17,64,512]{2,1,0:T(8,128)(2,1)S(1)}, bf16[17,64,512]{2,1,0:T(8,128)(2,1)S(1)}, u32[]{:S(2)}, u32[]{:S(2)}) %collective-permute-start.13) | collective-permute-done | bytes 1114144 | tf_op jit(solution)/shard_map/ppermute | solution.py:25
  102.7 6.4 %refresh_attend.1 = (bf16[512,512]{1,0:T(8,128)(2,1)}, bf16[512,512]{1,0:T(8,128)(2,1)}, bf16[256,640]{1,0:T(8,128)(2,1)S(1)}, bf16[256,640]{1,0:T(8,128)(2,1)S(1)}) custom-call(s32[8]{0:T(128)S(1)} %concatenate.3.pos.refs_0_, bf16[512,512]{1,0:T(8,128)(2,1)S(1)} %copy-done.3, bf16[512,512]{1,0:T(8,128)(2,1)S(1)} %copy-done.4, bf16[8,512]{1,0:T(8,128)(2,1)S(1)} %copy-done.7, ...), custom_call_target="tpu_custom_call" | custom-call | flops 3221225472 | bytes 12582912 | tf_op jit(solution)/shard_map/refresh_attend/pallas_call | solution.py:280
  109.2 2.3 %collective-permute-start.14 = (bf16[256,640]{1,0:T(8,128)(2,1)S(1)}, bf16[256,640]{1,0:T(8,128)(2,1)S(1)}, u32[]{:S(2)}, u32[]{:S(2)}) collective-permute-start(bf16[256,640]{1,0:T(8,128)(2,1)S(1)} %get-tuple-element.22), channel_id=1, source_target_pairs={{0,8},{8,0},{16,24},{24,16},{32,40},{40,32},{48,56},{56,48},{64,72... | collective-permute-start | bytes 983048 | tf_op jit(solution)/shard_map/ppermute | solution.py:25
  111.4 1.2 collective-permute-done.14.two
  112.7 1.0 merge.1
  113.7 19.5 %all_to_all.11 = bf16[32,8,640]{2,1,0:T(8,128)(2,1)S(1)} all-to-all(bf16[32,8,640]{2,1,0:T(8,128)(2,1)S(1)} %bitcast.9), channel_id=1, replica_groups={{0,64,128,192,256,320,384,448,16,80,144,208,272,336,400,464,32,96,160,2..., dimensions={0} | all-to-all | bytes 655360 | tf_op jit(solution)/shard_map/all_to_all | solution.py:323
  133.2 1.2 combine.1
  (24 shorter events, 0.1 us)
Async XLA Ops:
  7.2 31.3 %copy-start = (s32[64,4]{0,1:T(4,128)S(1)}, s32[64,4]{0,1:T(4,128)}, u32[]{:S(2)}) copy-start(s32[64,4]{0,1:T(4,128)} %param.20) | copy-start | bytes 3076
  7.2 73.8 %all-gather.3.cloned.1.call-start = ((), (), s32[]{:S(2)}) async-start(), calls=%async_computation.1 | async-start | bytes 4718592 | tf_op jit(solution)/shard_map/all_gather | solution.py:214
  7.9 0.8 copy-start.5
  8.8 0.8 copy-start.6
  9.6 0.7 copy-start.9
  10.3 20.6 %collective-permute-start.3 = (bf16[136,512]{1,0:T(8,128)(2,1)S(1)}, bf16[136,512]{1,0:T(8,128)(2,1)S(1)}, u32[]{:S(2)}, u32[]{:S(2)}) collective-permute-start(bf16[136,512]{1,0:T(8,128)(2,1)S(1)} %payload.1.refs_0_), channel_id=1, source_target_pairs={{0,192},{8,200},{16,208},{24,216},{32,224},{40,232},{48,240},{56,2... | collective-permute-start | bytes 417800 | tf_op jit(solution)/shard_map/ppermute | solution.py:25
  17.0 17.2 %collective-permute-start = (bf16[136,512]{1,0:T(8,128)(2,1)S(1)}, bf16[136,512]{1,0:T(8,128)(2,1)S(1)}, u32[]{:S(2)}, u32[]{:S(2)}) collective-permute-start(bf16[136,512]{1,0:T(8,128)(2,1)S(1)} %payload.1.refs_0_), channel_id=1, source_target_pairs={{0,448},{8,456},{16,464},{24,472},{32,480},{40,488},{48,496},{56,5... | collective-permute-start | bytes 417800 | tf_op jit(solution)/shard_map/ppermute | solution.py:25
  19.0 20.6 %collective-permute-start.1 = (bf16[136,512]{1,0:T(8,128)(2,1)S(1)}, bf16[136,512]{1,0:T(8,128)(2,1)S(1)}, u32[]{:S(2)}, u32[]{:S(2)}) collective-permute-start(bf16[136,512]{1,0:T(8,128)(2,1)S(1)} %payload.1.refs_0_), channel_id=1, source_target_pairs={{0,384},{8,392},{16,400},{24,408},{32,416},{40,424},{48,432},{56,4... | collective-permute-start | bytes 417800 | tf_op jit(solution)/shard_map/ppermute | solution.py:25
  21.7 18.0 %collective-permute-start.2 = (bf16[136,512]{1,0:T(8,128)(2,1)S(1)}, bf16[136,512]{1,0:T(8,128)(2,1)S(1)}, u32[]{:S(2)}, u32[]{:S(2)}) collective-permute-start(bf16[136,512]{1,0:T(8,128)(2,1)S(1)} %payload.1.refs_0_), channel_id=1, source_target_pairs={{0,320},{8,328},{16,336},{24,344},{32,352},{40,360},{48,368},{56,3... | collective-permute-start | bytes 417800 | tf_op jit(solution)/shard_map/ppermute | solution.py:25
  27.7 12.5 %collective-permute-start.5 = (bf16[136,512]{1,0:T(8,128)(2,1)S(1)}, bf16[136,512]{1,0:T(8,128)(2,1)S(1)}, u32[]{:S(2)}, u32[]{:S(2)}) collective-permute-start(bf16[136,512]{1,0:T(8,128)(2,1)S(1)} %payload.1.refs_0_), channel_id=1, source_target_pairs={{0,128},{8,136},{16,144},{24,152},{32,160},{40,168},{48,176},{56,1... | collective-permute-start | bytes 417800 | tf_op jit(solution)/shard_map/ppermute | solution.py:25
  30.9 9.8 %collective-permute-start.6 = (bf16[136,512]{1,0:T(8,128)(2,1)S(1)}, bf16[136,512]{1,0:T(8,128)(2,1)S(1)}, u32[]{:S(2)}, u32[]{:S(2)}) collective-permute-start(bf16[136,512]{1,0:T(8,128)(2,1)S(1)} %payload.1.refs_0_), channel_id=1, source_target_pairs={{0,64},{8,72},{16,80},{24,88},{32,96},{40,104},{48,112},{56,120},{... | collective-permute-start | bytes 417800 | tf_op jit(solution)/shard_map/ppermute | solution.py:25
  34.3 8.7 %collective-permute-start.4 = (bf16[136,512]{1,0:T(8,128)(2,1)S(1)}, bf16[136,512]{1,0:T(8,128)(2,1)S(1)}, u32[]{:S(2)}, u32[]{:S(2)}) collective-permute-start(bf16[136,512]{1,0:T(8,128)(2,1)S(1)} %collective-permute-done.3.refs_5_), channel_id=1, source_target_pairs={{0,64},{8,72},{16,80},{24,88},{32,96},{40,104},{48,112},{56,120},{... | collective-permute-start | bytes 417800 | tf_op jit(solution)/shard_map/ppermute | solution.py:25
  43.6 28.1 %collective-permute-start.8 = (bf16[17,64,512]{2,1,0:T(8,128)(2,1)S(1)}, bf16[17,64,512]{2,1,0:T(8,128)(2,1)S(1)}, u32[]{:S(2)}, u32[]{:S(2)}) collective-permute-start(bf16[17,64,512]{2,1,0:T(8,128)(2,1)S(1)} %get-tuple-element.14.own.refs_7_), channel_id=1, source_target_pairs={{0,48},{8,56},{16,0},{24,8},{32,16},{40,24},{48,32},{56,40},{64,11... | collective-permute-start | bytes 3342344 | tf_op jit(solution)/shard_map/ppermute | solution.py:25
  48.3 29.9 %collective-permute-start.9 = (bf16[17,64,512]{2,1,0:T(8,128)(2,1)S(1)}, bf16[17,64,512]{2,1,0:T(8,128)(2,1)S(1)}, u32[]{:S(2)}, u32[]{:S(2)}) collective-permute-start(bf16[17,64,512]{2,1,0:T(8,128)(2,1)S(1)} %get-tuple-element.14.own.refs_7_), channel_id=1, source_target_pairs={{0,16},{8,24},{16,32},{24,40},{32,48},{40,56},{48,0},{56,8},{64,80... | collective-permute-start | bytes 3342344 | tf_op jit(solution)/shard_map/ppermute | solution.py:25
  50.2 30.8 %collective-permute-start.7 = (bf16[17,64,512]{2,1,0:T(8,128)(2,1)S(1)}, bf16[17,64,512]{2,1,0:T(8,128)(2,1)S(1)}, u32[]{:S(2)}, u32[]{:S(2)}) collective-permute-start(bf16[17,64,512]{2,1,0:T(8,128)(2,1)S(1)} %get-tuple-element.14.own.refs_7_), channel_id=1, source_target_pairs={{0,8},{8,0},{16,24},{24,16},{32,40},{40,32},{48,56},{56,48},{64,72... | collective-permute-start | bytes 3342344 | tf_op jit(solution)/shard_map/ppermute | solution.py:25
  71.7 7.3 %copy-start.1 = (bf16[17,64,512]{2,1,0:T(8,128)(2,1)}, bf16[17,64,512]{2,1,0:T(8,128)(2,1)S(1)}, u32[]{:S(2)}) copy-start(bf16[17,64,512]{2,1,0:T(8,128)(2,1)S(1)} %collective-permute-done.8.following.refs_0_) | copy-start | bytes 3342340
  72.6 22.0 %collective-permute-start.11 = (bf16[9,64,512]{2,1,0:T(8,128)(2,1)}, bf16[9,64,512]{2,1,0:T(8,128)(2,1)}, u32[]{:S(2)}, u32[]{:S(2)}) collective-permute-start(bf16[9,64,512]{2,1,0:T(8,128)(2,1)} %part.3), channel_id=1, source_target_pairs={{0,48},{8,56},{16,0},{24,8},{32,16},{40,24},{48,32},{56,40},{64,11... | collective-permute-start | bytes 1769480 | tf_op jit(solution)/shard_map/ppermute | solution.py:25
  79.0 15.5 %collective-permute-start.10 = (bf16[8,64,512]{2,1,0:T(8,128)(2,1)}, bf16[8,64,512]{2,1,0:T(8,128)(2,1)}, u32[]{:S(2)}, u32[]{:S(2)}) collective-permute-start(bf16[8,64,512]{2,1,0:T(8,128)(2,1)} %part.2), channel_id=1, source_target_pairs={{0,16},{8,24},{16,32},{24,40},{32,48},{40,56},{48,0},{56,8},{64,80... | collective-permute-start | bytes 1572872 | tf_op jit(solution)/shard_map/ppermute | solution.py:25
  81.0 1.2 copy-start.2
  82.3 2.2 %copy-start.10 = (bf16[4096,512]{1,0:T(8,128)(2,1)S(1)}, bf16[4096,512]{1,0:T(8,128)(2,1)}, u32[]{:S(2)}) copy-start(bf16[4096,512]{1,0:T(8,128)(2,1)} %all-gather.3.cloned.1.call-done) | copy-start | bytes 12582916
  94.6 8.2 %copy-start.3 = (bf16[512,512]{1,0:T(8,128)(2,1)S(1)}, bf16[512,512]{1,0:T(8,128)(2,1)}, u32[]{:S(2)}) copy-start(bf16[512,512]{1,0:T(8,128)(2,1)} %refs_1_.1) | copy-start | bytes 1572868
  94.6 8.2 %copy-start.4 = (bf16[512,512]{1,0:T(8,128)(2,1)S(1)}, bf16[512,512]{1,0:T(8,128)(2,1)}, u32[]{:S(2)}) copy-start(bf16[512,512]{1,0:T(8,128)(2,1)} %refs_2_.1) | copy-start | bytes 1572868
  94.6 8.2 %copy-start.7 = (bf16[8,512]{1,0:T(8,128)(2,1)S(1)}, bf16[8,512]{1,0:T(8,128)(2,1)}, u32[]{:S(2)}) copy-start(bf16[8,512]{1,0:T(8,128)(2,1)} %refs_3_.1) | copy-start | bytes 24580
  94.6 8.2 %copy-start.8 = (bf16[8,512]{1,0:T(8,128)(2,1)S(1)}, bf16[8,512]{1,0:T(8,128)(2,1)}, u32[]{:S(2)}) copy-start(bf16[8,512]{1,0:T(8,128)(2,1)} %refs_4_.1) | copy-start | bytes 24580
  94.6 8.1 %collective-permute-start.12 = (bf16[2,17,64,512]{3,2,1,0:T(8,128)(2,1)S(1)}, bf16[2,17,64,512]{3,2,1,0:T(8,128)(2,1)S(1)}, u32[]{:S(2)}, u32[]{:S(2)}) collective-permute-start(bf16[2,17,64,512]{3,2,1,0:T(8,128)(2,1)S(1)} %get-tuple-element.18.refs_9_), channel_id=1, source_target_pairs={{0,8},{8,0},{16,24},{24,16},{32,40},{40,32},{48,56},{56,48},{64,72... | collective-permute-start | bytes 6684680 | tf_op jit(solution)/shard_map/ppermute | solution.py:25
  98.0 4.8 %collective-permute-start.13 = (bf16[17,64,512]{2,1,0:T(8,128)(2,1)S(1)}, bf16[17,64,512]{2,1,0:T(8,128)(2,1)S(1)}, u32[]{:S(2)}, u32[]{:S(2)}) collective-permute-start(bf16[17,64,512]{2,1,0:T(8,128)(2,1)S(1)} %join.1.refs_11_), channel_id=1, source_target_pairs={{0,8},{8,0},{16,24},{24,16},{32,40},{40,32},{48,56},{56,48},{64,72... | collective-permute-start | bytes 3342344 | tf_op jit(solution)/shard_map/ppermute | solution.py:25
  109.2 3.5 %collective-permute-start.14 = (bf16[256,640]{1,0:T(8,128)(2,1)S(1)}, bf16[256,640]{1,0:T(8,128)(2,1)S(1)}, u32[]{:S(2)}, u32[]{:S(2)}) collective-permute-start(bf16[256,640]{1,0:T(8,128)(2,1)S(1)} %get-tuple-element.22), channel_id=1, source_target_pairs={{0,8},{8,0},{16,24},{24,16},{32,40},{40,32},{48,56},{56,48},{64,72... | collective-permute-start | bytes 983048 | tf_op jit(solution)/shard_map/ppermute | solution.py:25
Sparse Core Ops, SparseCore 0:
  10.1 55.7 all-gather.2
